TPU v7x, 256 devices: a whole 4x4x8 slice. The times are simulated.
256 devices in a mesh: gx: 32 (over x, z), gy: 8 (over y, core).
Axes of the slice: x: 4, y: 4, z: 8, core: 2. Of those that a mesh axis runs over, the one named last changes fastest.
Arguments:
- vorticity: float32 [8, 512, 1024], P(None, 'gx', 'gy'), may hold values from -6 to 6
- metric: float32 [3, 8, 512, 1024], P(None, None, 'gx', 'gy'), may hold values from 0.25 to 4
Outputs:
- stream: float32 [8, 512, 1024], P(None, 'gx', 'gy')
- residual: float32 [8, 512, 1024], P(None, 'gx', 'gy')
All inputs are finite; a program needn't handle non-finite values.
Results may differ from a plain program's by a relative error of at most 0.0003.
Values sent between devices are 32-bit elements; how exact they have to be, the bound alone decides.
A program may use at most 64 MiB of HBM per device.

v0:
```python
import jax
import jax.numpy as jnp
from jax import lax
from jax.sharding import PartitionSpec as P

LEVELS = 5
CSWEEPS = 8


omega_relax = 0.8


def extended(x, sides, width):
    for axis, dim in sides:
        count, length = (lax.axis_size(axis), x.shape[dim])
        up = [(i, (i + 1) % count) for i in range(count - 1)]
        down = [(j, i) for i, j in up]
        last = lax.slice_in_dim(x, length - width, length, axis=dim)
        leading = lax.slice_in_dim(x, 0, width, axis=dim)
        before = lax.ppermute(last, axis, up)
        after = lax.ppermute(leading, axis, down)
        x = jnp.concatenate([before, x, after], axis=dim)
    return x


def coarsen(values):
    shape = values.shape
    grouped = values.reshape(shape[:-2] + (shape[-2] // 2, 2, shape[-1] // 2, 2))
    return grouped.mean(axis=(-3, -1))


def refine(values):
    return jnp.repeat(jnp.repeat(values, 2, axis=1), 2, axis=2)


def face_coeffs(metric, padded, level_no):
    scale = 0.25**level_no
    span_scale = 0.25 ** (LEVELS - 1)
    m_x = metric[0]
    m_y = metric[1]
    m_z = metric[2]
    c_east = 0.5 * (m_x + padded[0, :, 2:, 1:-1]) * scale
    c_west = 0.5 * (m_x + padded[0, :, :-2, 1:-1]) * scale
    c_north = 0.5 * (m_y + padded[1, :, 1:-1, 2:]) * scale
    c_south = 0.5 * (m_y + padded[1, :, 1:-1, :-2]) * scale
    c_upper = 0.5 * (m_z + jnp.roll(m_z, -1, 0)) * span_scale
    c_lower = 0.5 * (m_z + jnp.roll(m_z, 1, 0)) * span_scale
    c_diag = c_east + c_west + c_north + c_south + c_upper + c_lower
    return (c_east, c_west, c_north, c_south, c_upper, c_lower, c_diag)


def stencil(field, padded, coeffs):
    beside = coeffs[0] * padded[:, 2:, 1:-1] + coeffs[1] * padded[:, :-2, 1:-1]
    beside = beside + coeffs[2] * padded[:, 1:-1, 2:] + coeffs[3] * padded[:, 1:-1, :-2]
    beside = beside + coeffs[4] * jnp.roll(field, -1, 0) + coeffs[5] * jnp.roll(field, 1, 0)
    return coeffs[6] * field - beside


def local_apply(field, coeffs):
    padded = jnp.pad(field, ((0, 0), (1, 1), (1, 1)))
    return stencil(field, padded, coeffs)


def shared_apply(field, coeffs):
    padded = extended(field, (("gx", 1), ("gy", 2)), 1)
    return stencil(field, padded, coeffs)


def shared_coeffs(metric, level_no):
    padded = extended(metric[:2], (("gx", 2), ("gy", 3)), 1)
    return face_coeffs(metric, padded, level_no)


def local_total(values):
    return jnp.sum(values)


def collect(stacked):
    gathered = lax.all_gather(stacked, "gy", axis=3, tiled=True)
    return lax.all_gather(gathered, "gx", axis=2, tiled=True)


def relax_all(field, source, coeffs, sweeps, apply_fn):
    for sweep_no in range(sweeps):
        field = field + omega_relax * (source - apply_fn(field, coeffs)) / coeffs[6]
    return field


def coarse_solve(source, coeffs, apply_fn, total_fn):
    field = jnp.zeros_like(source)
    resid = source
    direction = source
    norm_now = total_fn(resid * resid)
    for sweep_no in range(CSWEEPS):
        image = apply_fn(direction, coeffs)
        alpha = norm_now / total_fn(direction * image)
        field = field + alpha * direction
        resid = resid - alpha * image
        if sweep_no + 1 < CSWEEPS:
            norm_next = total_fn(resid * resid)
            direction = resid + norm_next / norm_now * direction
            norm_now = norm_next
    return field


def v_cycle(source, level_no, levels, coarse_coeffs):
    if level_no == LEVELS - 1:
        depth_z, rows_x, rows_y = source.shape
        whole_source = collect(source[None])[0]
        field = coarse_solve(whole_source, coarse_coeffs, local_apply, local_total)
        start_x = lax.axis_index("gx") * rows_x
        start_y = lax.axis_index("gy") * rows_y
        return lax.dynamic_slice(field, (jnp.int32(0), start_x, start_y), (depth_z, rows_x, rows_y))
    inner, loop, inside = levels[level_no]
    field = omega_relax * source / inner[6]
    field = relax_all(field, source, inner, 1, shared_apply)
    remains = source - shared_apply(field, inner)
    field = field + refine(v_cycle(coarsen(remains), level_no + 1, levels, coarse_coeffs))
    return relax_all(field, source, inner, 2, shared_apply)


def on_device(vorticity, metric):
    metrics = [metric]
    for level_no in range(1, LEVELS):
        metrics.append(coarsen(metrics[-1]))
    spread = LEVELS - 1
    levels = []
    for level_no in range(spread):
        levels.append((shared_coeffs(metrics[level_no], level_no), None, None))
    coarse_coeffs = None
    gathered = collect(metrics[-1])
    padded = jnp.pad(gathered[:2], ((0, 0), (0, 0), (1, 1), (1, 1)))
    coarse_coeffs = face_coeffs(gathered, padded, LEVELS - 1)
    stream = v_cycle(vorticity, 0, levels, coarse_coeffs)
    residual = vorticity - shared_apply(stream, levels[0][0])
    return (stream, residual)


def solution(mesh):
    placed = (P(None, "gx", "gy"), P(None, None, "gx", "gy"))
    return jax.shard_map(
        on_device,
        mesh=mesh,
        in_specs=placed,
        out_specs=(P(None, "gx", "gy"), P(None, "gx", "gy")),
        check_vma=False,
    )
```

profile of v0, /device:TPU:1, one launch (start us, length us, event | category | flops | bytes accessed | tf_op | source)
XLA Modules:
  0.0 576.7 jit_solution(16341017975946171434)
XLA Ops:
  2.1 5.0 collective-permute-start.1
  10.2 3.9 reduce_sum.231
  16.2 4.0 collective-permute-start.13
  23.3 4.6 collective-permute-start.37
  34.4 15.2 %all-gather.2 = f32[3,8,64]{1,0,2:T(4,128)S(1)} all-gather(f32[3,8,8]{1,0,2:T(4,128)S(1)} %copy.1448), channel_id=4, replica_groups=mesh['gx'=32,'gy'=8] {'gy'}, dimensions={2}, use_global_device_ids=true | all-gather | bytes 6912 | tf_op jit(solution)/shard_map/all_gather | solution.py:79
  49.6 48.5 %all-gather.3 = f32[3,8,2048]{1,0,2:T(4,128)S(1)} all-gather(f32[3,8,64]{1,0,2:T(4,128)S(1)} %all-gather.2), channel_id=5, replica_groups=mesh['gx'=32,'gy'=8] {'gx'}, dimensions={2}, use_global_device_ids=true | all-gather | bytes 202752 | tf_op jit(solution)/shard_map/all_gather | solution.py:80
  98.2 3.7 fusion.385
  101.9 4.6 fusion.386
  106.5 4.2 fusion.387
  119.5 3.4 copy.1526
  122.9 3.4 copy.1529
  126.3 3.4 copy.1527
  139.8 14.0 %collective-permute-start.38 = (f32[2,8,4,1]{1,3,2,0:T(1,128)}, f32[2,8,4,1]{1,3,2,0:T(1,128)}, u32[]{:S(2)}, u32[]{:S(2)}) collective-permute-start(f32[2,8,4,1]{1,3,2,0:T(1,128)} %get-tuple-element.196), channel_id=1, source_target_pairs={{1,0},{2,1},{3,2},{4,3},{5,4},{6,5},{7,6},{9,8},{10,9},{11,10},{12... | collective-permute-start | bytes 776 | tf_op jit(solution)/shard_map/ppermute | solution.py:21
  156.6 3.6 collective-permute-start.27
  163.2 3.6 collective-permute-start.15
  173.6 3.0 collective-permute-start.2
  183.5 4.2 collective-permute-start.5
  190.2 5.5 collective-permute-start.7
  197.4 4.0 collective-permute-start.9
  202.8 3.0 collective-permute-done.8
  207.8 5.7 collective-permute-start.11
  216.6 4.0 collective-permute-start.17
  221.9 4.8 collective-permute-done.16
  228.7 5.4 collective-permute-start.19
  235.4 4.8 collective-permute-start.21
  241.6 3.3 collective-permute-done.20
  246.9 5.4 collective-permute-start.23
  255.2 3.6 collective-permute-start.29
  260.4 3.0 collective-permute-done.28
  265.4 5.7 collective-permute-start.31
  272.4 4.8 collective-permute-start.33
  278.7 3.2 collective-permute-done.32
  284.0 5.4 collective-permute-start.35
  293.0 5.5 collective-permute-start.41
  301.1 5.1 collective-permute-start.43
  308.3 4.6 collective-permute-start.45
  315.6 5.0 collective-permute-start.47
  321.5 13.9 %all-gather = f32[8,64]{0,1:T(8,128)S(1)} all-gather(f32[8,8]{0,1:T(8,128)S(1)} %broadcast_multiply_fusion.5), channel_id=2, replica_groups=mesh['gx'=32,'gy'=8] {'gy'}, dimensions={1}, use_global_device_ids=true | all-gather | bytes 2304 | tf_op jit(solution)/shard_map/all_gather | solution.py:79
  335.5 43.2 %all-gather.4 = f32[32,64,8]{1,2,0:T(8,128)S(1)} all-gather(f32[1,64,8]{1,2,0:T(8,128)S(1)} %copy.1444), channel_id=3, replica_groups=mesh['gx'=32,'gy'=8] {'gx'}, dimensions={0}, use_global_device_ids=true | all-gather | bytes 67584 | tf_op jit(solution)/shard_map/all_gather | solution.py:80
  415.7 4.0 collective-permute-start.49
  420.5 13.2 %collective-permute-start.50 = (f32[8,4,1]{0,2,1:T(1,128)S(1)}, f32[8,4,1]{0,2,1:T(1,128)S(1)}, u32[]{:S(2)}, u32[]{:S(2)}) collective-permute-start(f32[8,4,1]{0,2,1:T(1,128)S(1)} %get-tuple-element.263), channel_id=1, source_target_pairs={{1,0},{2,1},{3,2},{4,3},{5,4},{6,5},{7,6},{9,8},{10,9},{11,10},{12... | collective-permute-start | bytes 392 | tf_op jit(solution)/shard_map/ppermute | solution.py:21
  438.1 4.6 collective-permute-start.53
  446.4 3.7 collective-permute-start.55
  451.0 3.9 collective-permute-start.57
  456.5 3.2 collective-permute-done.56
  461.8 5.3 collective-permute-start.59
  468.4 3.6 collective-permute-start.61
  473.6 3.0 collective-permute-done.60
  478.6 5.6 collective-permute-start.63
  486.0 4.1 collective-permute-start.65
  491.4 3.3 collective-permute-done.64
  496.7 5.6 collective-permute-start.67
  503.4 3.6 collective-permute-start.69
  508.4 3.1 collective-permute-done.68
  513.5 5.5 collective-permute-start.71
  520.8 5.6 collective-permute-start.73
  527.7 3.3 collective-permute-done.72
  533.0 5.4 collective-permute-start.75
  540.0 4.8 collective-permute-start.77
  546.3 3.3 collective-permute-done.76
  551.5 5.4 collective-permute-start.79
  558.6 3.7 collective-permute-start.81
  563.7 3.3 collective-permute-done.80
  569.0 5.4 collective-permute-start.83
  (460 shorter events, 156.1 us)
Async XLA Ops:
  2.1 169.9 %collective-permute-start.1 = (f32[2,8,1,128]{3,1,2,0:T(8,128)}, f32[2,8,1,128]{3,1,2,0:T(8,128)}, u32[]{:S(2)}, u32[]{:S(2)}) collective-permute-start(f32[2,8,1,128]{3,1,2,0:T(8,128)} %bitcast.94), channel_id=1, source_target_pairs={{0,8},{8,16},{16,24},{24,32},{32,40},{40,48},{48,56},{56,64},{64,7... | collective-permute-start | bytes 24584 | tf_op jit(solution)/shard_map/ppermute | solution.py:20
  7.1 165.7 %collective-permute-start = (f32[2,8,1,128]{3,1,2,0:T(8,128)}, f32[2,8,1,128]{3,1,2,0:T(8,128)}, u32[]{:S(2)}, u32[]{:S(2)}) collective-permute-start(f32[2,8,1,128]{3,1,2,0:T(8,128)} %bitcast.93), channel_id=1, source_target_pairs={{8,0},{16,8},{24,16},{32,24},{40,32},{48,40},{56,48},{64,56},{72,6... | collective-permute-start | bytes 24584 | tf_op jit(solution)/shard_map/ppermute | solution.py:21
  16.2 138.4 %collective-permute-start.13 = (f32[2,8,1,64]{3,2,1,0:T(1,128)}, f32[2,8,1,64]{3,2,1,0:T(1,128)S(1)}, u32[]{:S(2)}, u32[]{:S(2)}) collective-permute-start(f32[2,8,1,64]{3,2,1,0:T(1,128)} %get-tuple-element.140), channel_id=1, source_target_pairs={{0,8},{8,16},{16,24},{24,32},{32,40},{40,48},{48,56},{56,64},{64,7... | collective-permute-start | bytes 12296 | tf_op jit(solution)/shard_map/ppermute | solution.py:20
  22.0 110.3 %collective-permute-start.36 = (f32[2,8,1,16]{1,3,2,0:T(8,128)}, f32[2,8,1,16]{1,3,2,0:T(8,128)}, u32[]{:S(2)}, u32[]{:S(2)}) collective-permute-start(f32[2,8,1,16]{1,3,2,0:T(8,128)} %get-tuple-element.227), channel_id=1, source_target_pairs={{8,0},{16,8},{24,16},{32,24},{40,32},{48,40},{56,48},{64,56},{72,6... | collective-permute-start | bytes 3080 | tf_op jit(solution)/shard_map/ppermute | solution.py:21
  23.3 111.6 %collective-permute-start.37 = (f32[2,8,1,16]{1,3,2,0:T(8,128)}, f32[2,8,1,16]{1,3,2,0:T(8,128)}, u32[]{:S(2)}, u32[]{:S(2)}) collective-permute-start(f32[2,8,1,16]{1,3,2,0:T(8,128)} %get-tuple-element.228), channel_id=1, source_target_pairs={{0,8},{8,16},{16,24},{24,32},{32,40},{40,48},{48,56},{56,64},{64,7... | collective-permute-start | bytes 3080 | tf_op jit(solution)/shard_map/ppermute | solution.py:20
  132.3 5.3 collective-permute-start.25
  137.6 19.0 %collective-permute-start.12 = (f32[2,8,1,64]{3,2,1,0:T(1,128)}, f32[2,8,1,64]{3,2,1,0:T(1,128)S(1)}, u32[]{:S(2)}, u32[]{:S(2)}) collective-permute-start(f32[2,8,1,64]{3,2,1,0:T(1,128)} %get-tuple-element.139), channel_id=1, source_target_pairs={{8,0},{16,8},{24,16},{32,24},{40,32},{48,40},{56,48},{64,56},{72,6... | collective-permute-start | bytes 12296 | tf_op jit(solution)/shard_map/ppermute | solution.py:21
  139.8 151.0 %collective-permute-start.38 = (f32[2,8,4,1]{1,3,2,0:T(1,128)}, f32[2,8,4,1]{1,3,2,0:T(1,128)}, u32[]{:S(2)}, u32[]{:S(2)}) collective-permute-start(f32[2,8,4,1]{1,3,2,0:T(1,128)} %get-tuple-element.196), channel_id=1, source_target_pairs={{1,0},{2,1},{3,2},{4,3},{5,4},{6,5},{7,6},{9,8},{10,9},{11,10},{12... | collective-permute-start | bytes 776 | tf_op jit(solution)/shard_map/ppermute | solution.py:21
  154.7 6.5 %collective-permute-start.26 = (f32[2,8,6,1]{3,1,2,0:T(8,128)S(1)}, f32[2,8,6,1]{3,1,2,0:T(8,128)S(1)}, u32[]{:S(2)}, u32[]{:S(2)}) collective-permute-start(f32[2,8,6,1]{3,1,2,0:T(8,128)S(1)} %get-tuple-element.232), channel_id=1, source_target_pairs={{1,0},{2,1},{3,2},{4,3},{5,4},{6,5},{7,6},{9,8},{10,9},{11,10},{12... | collective-permute-start | bytes 1160 | tf_op jit(solution)/shard_map/ppermute | solution.py:21
  156.6 6.5 %collective-permute-start.27 = (f32[2,8,6,1]{3,1,2,0:T(8,128)S(1)}, f32[2,8,6,1]{3,1,2,0:T(8,128)S(1)}, u32[]{:S(2)}, u32[]{:S(2)}) collective-permute-start(f32[2,8,6,1]{3,1,2,0:T(8,128)S(1)} %get-tuple-element.231), channel_id=1, source_target_pairs={{0,1},{1,2},{2,3},{3,4},{4,5},{5,6},{6,7},{8,9},{9,10},{10,11},{11... | collective-permute-start | bytes 1160 | tf_op jit(solution)/shard_map/ppermute | solution.py:20
  161.2 7.9 %collective-permute-start.14 = (f32[2,8,10,1]{3,1,2,0:T(8,128)S(1)}, f32[2,8,10,1]{3,1,2,0:T(8,128)S(1)}, u32[]{:S(2)}, u32[]{:S(2)}) collective-permute-start(f32[2,8,10,1]{3,1,2,0:T(8,128)S(1)} %get-tuple-element.144), channel_id=1, source_target_pairs={{1,0},{2,1},{3,2},{4,3},{5,4},{6,5},{7,6},{9,8},{10,9},{11,10},{12... | collective-permute-start | bytes 1928 | tf_op jit(solution)/shard_map/ppermute | solution.py:21
  163.2 7.9 %collective-permute-start.15 = (f32[2,8,10,1]{3,1,2,0:T(8,128)S(1)}, f32[2,8,10,1]{3,1,2,0:T(8,128)S(1)}, u32[]{:S(2)}, u32[]{:S(2)}) collective-permute-start(f32[2,8,10,1]{3,1,2,0:T(8,128)S(1)} %get-tuple-element.143), channel_id=1, source_target_pairs={{0,1},{1,2},{2,3},{3,4},{4,5},{5,6},{6,7},{8,9},{9,10},{10,11},{11... | collective-permute-start | bytes 1928 | tf_op jit(solution)/shard_map/ppermute | solution.py:20
  169.1 121.6 %collective-permute-start.39 = (f32[2,8,4,1]{1,3,2,0:T(1,128)}, f32[2,8,4,1]{1,3,2,0:T(1,128)}, u32[]{:S(2)}, u32[]{:S(2)}) collective-permute-start(f32[2,8,4,1]{1,3,2,0:T(1,128)} %get-tuple-element.195), channel_id=1, source_target_pairs={{0,1},{1,2},{2,3},{3,4},{4,5},{5,6},{6,7},{8,9},{9,10},{10,11},{11... | collective-permute-start | bytes 776 | tf_op jit(solution)/shard_map/ppermute | solution.py:20
  173.6 6.5 %collective-permute-start.2 = (f32[2,8,18,1]{3,1,2,0:T(8,128)S(1)}, f32[2,8,18,1]{3,1,2,0:T(8,128)S(1)}, u32[]{:S(2)}, u32[]{:S(2)}) collective-permute-start(f32[2,8,18,1]{3,1,2,0:T(8,128)S(1)} %get-tuple-element.95), channel_id=1, source_target_pairs={{1,0},{2,1},{3,2},{4,3},{5,4},{6,5},{7,6},{9,8},{10,9},{11,10},{12... | collective-permute-start | bytes 3464 | tf_op jit(solution)/shard_map/ppermute | solution.py:21
  182.2 5.6 collective-permute-start.4
  188.3 7.5 %collective-permute-start.6 = (f32[8,18,1]{2,0,1:T(8,128)S(1)}, f32[8,18,1]{2,0,1:T(8,128)S(1)}, u32[]{:S(2)}, u32[]{:S(2)}) collective-permute-start(f32[8,18,1]{2,0,1:T(8,128)S(1)} %get-tuple-element.163), channel_id=1, source_target_pairs={{1,0},{2,1},{3,2},{4,3},{5,4},{6,5},{7,6},{9,8},{10,9},{11,10},{12... | collective-permute-start | bytes 1736 | tf_op jit(solution)/shard_map/ppermute | solution.py:21
  190.2 6.9 %collective-permute-start.7 = (f32[8,18,1]{2,0,1:T(8,128)S(1)}, f32[8,18,1]{2,0,1:T(8,128)S(1)}, u32[]{:S(2)}, u32[]{:S(2)}) collective-permute-start(f32[8,18,1]{2,0,1:T(8,128)S(1)} %get-tuple-element.164), channel_id=1, source_target_pairs={{0,1},{1,2},{2,3},{3,4},{4,5},{5,6},{6,7},{8,9},{9,10},{10,11},{11... | collective-permute-start | bytes 1736 | tf_op jit(solution)/shard_map/ppermute | solution.py:20
  197.4 5.4 collective-permute-start.9
  205.9 7.7 %collective-permute-start.10 = (f32[8,18,1]{2,0,1:T(8,128)S(1)}, f32[8,18,1]{2,0,1:T(8,128)S(1)}, u32[]{:S(2)}, u32[]{:S(2)}) collective-permute-start(f32[8,18,1]{2,0,1:T(8,128)S(1)} %get-tuple-element.159), channel_id=1, source_target_pairs={{1,0},{2,1},{3,2},{4,3},{5,4},{6,5},{7,6},{9,8},{10,9},{11,10},{12... | collective-permute-start | bytes 1736 | tf_op jit(solution)/shard_map/ppermute | solution.py:21
  207.8 7.1 %collective-permute-start.11 = (f32[8,18,1]{2,0,1:T(8,128)S(1)}, f32[8,18,1]{2,0,1:T(8,128)S(1)}, u32[]{:S(2)}, u32[]{:S(2)}) collective-permute-start(f32[8,18,1]{2,0,1:T(8,128)S(1)} %get-tuple-element.160), channel_id=1, source_target_pairs={{0,1},{1,2},{2,3},{3,4},{4,5},{5,6},{6,7},{8,9},{9,10},{10,11},{11... | collective-permute-start | bytes 1736 | tf_op jit(solution)/shard_map/ppermute | solution.py:20
  216.6 5.3 collective-permute-start.17
  220.5 6.1 %collective-permute-start.16 = (f32[8,1,64]{2,1,0:T(1,128)S(1)}, f32[8,1,64]{2,1,0:T(1,128)S(1)}, u32[]{:S(2)}, u32[]{:S(2)}) collective-permute-start(f32[8,1,64]{2,1,0:T(1,128)S(1)} %get-tuple-element.279), channel_id=1, source_target_pairs={{8,0},{16,8},{24,16},{32,24},{40,32},{48,40},{56,48},{64,56},{72,6... | collective-permute-start | bytes 6152 | tf_op jit(solution)/shard_map/ppermute | solution.py:21
  226.7 7.4 %collective-permute-start.18 = (f32[8,10,1]{2,0,1:T(8,128)S(1)}, f32[8,10,1]{2,0,1:T(8,128)S(1)}, u32[]{:S(2)}, u32[]{:S(2)}) collective-permute-start(f32[8,10,1]{2,0,1:T(8,128)S(1)} %get-tuple-element.247), channel_id=1, source_target_pairs={{1,0},{2,1},{3,2},{4,3},{5,4},{6,5},{7,6},{9,8},{10,9},{11,10},{12... | collective-permute-start | bytes 968 | tf_op jit(solution)/shard_map/ppermute | solution.py:21
  228.7 6.5 %collective-permute-start.19 = (f32[8,10,1]{2,0,1:T(8,128)S(1)}, f32[8,10,1]{2,0,1:T(8,128)S(1)}, u32[]{:S(2)}, u32[]{:S(2)}) collective-permute-start(f32[8,10,1]{2,0,1:T(8,128)S(1)} %get-tuple-element.248), channel_id=1, source_target_pairs={{0,1},{1,2},{2,3},{3,4},{4,5},{5,6},{6,7},{8,9},{9,10},{10,11},{11... | collective-permute-start | bytes 968 | tf_op jit(solution)/shard_map/ppermute | solution.py:20
  235.4 6.2 %collective-permute-start.21 = (f32[8,1,64]{2,1,0:T(1,128)S(1)}, f32[8,1,64]{2,1,0:T(1,128)S(1)}, u32[]{:S(2)}, u32[]{:S(2)}) collective-permute-start(f32[8,1,64]{2,1,0:T(1,128)S(1)} %get-tuple-element.274), channel_id=1, source_target_pairs={{0,8},{8,16},{16,24},{24,32},{32,40},{40,48},{48,56},{56,64},{64,7... | collective-permute-start | bytes 6152 | tf_op jit(solution)/shard_map/ppermute | solution.py:20
  244.9 7.3 %collective-permute-start.22 = (f32[8,10,1]{2,0,1:T(8,128)S(1)}, f32[8,10,1]{2,0,1:T(8,128)S(1)}, u32[]{:S(2)}, u32[]{:S(2)}) collective-permute-start(f32[8,10,1]{2,0,1:T(8,128)S(1)} %get-tuple-element.243), channel_id=1, source_target_pairs={{1,0},{2,1},{3,2},{4,3},{5,4},{6,5},{7,6},{9,8},{10,9},{11,10},{12... | collective-permute-start | bytes 968 | tf_op jit(solution)/shard_map/ppermute | solution.py:21
  246.9 6.5 %collective-permute-start.23 = (f32[8,10,1]{2,0,1:T(8,128)S(1)}, f32[8,10,1]{2,0,1:T(8,128)S(1)}, u32[]{:S(2)}, u32[]{:S(2)}) collective-permute-start(f32[8,10,1]{2,0,1:T(8,128)S(1)} %get-tuple-element.244), channel_id=1, source_target_pairs={{0,1},{1,2},{2,3},{3,4},{4,5},{5,6},{6,7},{8,9},{9,10},{10,11},{11... | collective-permute-start | bytes 968 | tf_op jit(solution)/shard_map/ppermute | solution.py:20
  263.5 7.7 %collective-permute-start.30 = (f32[8,6,1]{2,0,1:T(8,128)S(1)}, f32[8,6,1]{2,0,1:T(8,128)S(1)}, u32[]{:S(2)}, u32[]{:S(2)}) collective-permute-start(f32[8,6,1]{2,0,1:T(8,128)S(1)} %get-tuple-element.295), channel_id=1, source_target_pairs={{1,0},{2,1},{3,2},{4,3},{5,4},{6,5},{7,6},{9,8},{10,9},{11,10},{12... | collective-permute-start | bytes 584 | tf_op jit(solution)/shard_map/ppermute | solution.py:21
  265.4 6.6 %collective-permute-start.31 = (f32[8,6,1]{2,0,1:T(8,128)S(1)}, f32[8,6,1]{2,0,1:T(8,128)S(1)}, u32[]{:S(2)}, u32[]{:S(2)}) collective-permute-start(f32[8,6,1]{2,0,1:T(8,128)S(1)} %get-tuple-element.296), channel_id=1, source_target_pairs={{0,1},{1,2},{2,3},{3,4},{4,5},{5,6},{6,7},{8,9},{9,10},{10,11},{11... | collective-permute-start | bytes 584 | tf_op jit(solution)/shard_map/ppermute | solution.py:20
  272.4 6.2 %collective-permute-start.33 = (f32[8,1,32]{0,2,1:T(8,128)S(1)}, f32[8,1,32]{0,2,1:T(8,128)S(1)}, u32[]{:S(2)}, u32[]{:S(2)}) collective-permute-start(f32[8,1,32]{0,2,1:T(8,128)S(1)} %get-tuple-element.202), channel_id=1, source_target_pairs={{0,8},{8,16},{16,24},{24,32},{32,40},{40,48},{48,56},{56,64},{64,7... | collective-permute-start | bytes 3080 | tf_op jit(solution)/shard_map/ppermute | solution.py:20
  282.1 7.4 %collective-permute-start.34 = (f32[8,6,1]{2,0,1:T(8,128)S(1)}, f32[8,6,1]{2,0,1:T(8,128)S(1)}, u32[]{:S(2)}, u32[]{:S(2)}) collective-permute-start(f32[8,6,1]{2,0,1:T(8,128)S(1)} %get-tuple-element.291), channel_id=1, source_target_pairs={{1,0},{2,1},{3,2},{4,3},{5,4},{6,5},{7,6},{9,8},{10,9},{11,10},{12... | collective-permute-start | bytes 584 | tf_op jit(solution)/shard_map/ppermute | solution.py:21
  284.0 6.3 %collective-permute-start.35 = (f32[8,6,1]{2,0,1:T(8,128)S(1)}, f32[8,6,1]{2,0,1:T(8,128)S(1)}, u32[]{:S(2)}, u32[]{:S(2)}) collective-permute-start(f32[8,6,1]{2,0,1:T(8,128)S(1)} %get-tuple-element.292), channel_id=1, source_target_pairs={{0,1},{1,2},{2,3},{3,4},{4,5},{5,6},{6,7},{8,9},{9,10},{10,11},{11... | collective-permute-start | bytes 584 | tf_op jit(solution)/shard_map/ppermute | solution.py:20
  291.7 6.9 %collective-permute-start.40 = (f32[8,1,16]{0,2,1:T(8,128)S(1)}, f32[8,1,16]{0,2,1:T(8,128)S(1)}, u32[]{:S(2)}, u32[]{:S(2)}) collective-permute-start(f32[8,1,16]{0,2,1:T(8,128)S(1)} %get-tuple-element.320), channel_id=1, source_target_pairs={{8,0},{16,8},{24,16},{32,24},{40,32},{48,40},{56,48},{64,56},{72,6... | collective-permute-start | bytes 1544 | tf_op jit(solution)/shard_map/ppermute | solution.py:21
  293.0 6.3 %collective-permute-start.41 = (f32[8,1,16]{0,2,1:T(8,128)S(1)}, f32[8,1,16]{0,2,1:T(8,128)S(1)}, u32[]{:S(2)}, u32[]{:S(2)}) collective-permute-start(f32[8,1,16]{0,2,1:T(8,128)S(1)} %get-tuple-element.319), channel_id=1, source_target_pairs={{0,8},{8,16},{16,24},{24,32},{32,40},{40,48},{48,56},{56,64},{64,7... | collective-permute-start | bytes 1544 | tf_op jit(solution)/shard_map/ppermute | solution.py:20
  299.2 7.1 %collective-permute-start.42 = (f32[8,4,1]{0,2,1:T(1,128)S(1)}, f32[8,4,1]{0,2,1:T(1,128)S(1)}, u32[]{:S(2)}, u32[]{:S(2)}) collective-permute-start(f32[8,4,1]{0,2,1:T(1,128)S(1)} %get-tuple-element.267), channel_id=1, source_target_pairs={{1,0},{2,1},{3,2},{4,3},{5,4},{6,5},{7,6},{9,8},{10,9},{11,10},{12... | collective-permute-start | bytes 392 | tf_op jit(solution)/shard_map/ppermute | solution.py:21
  301.1 5.8 %collective-permute-start.43 = (f32[8,4,1]{0,2,1:T(1,128)S(1)}, f32[8,4,1]{0,2,1:T(1,128)S(1)}, u32[]{:S(2)}, u32[]{:S(2)}) collective-permute-start(f32[8,4,1]{0,2,1:T(1,128)S(1)} %get-tuple-element.268), channel_id=1, source_target_pairs={{0,1},{1,2},{2,3},{3,4},{4,5},{5,6},{6,7},{8,9},{9,10},{10,11},{11... | collective-permute-start | bytes 392 | tf_op jit(solution)/shard_map/ppermute | solution.py:20
  307.0 5.9 %collective-permute-start.44 = (f32[8,1,16]{0,2,1:T(8,128)S(1)}, f32[8,1,16]{0,2,1:T(8,128)S(1)}, u32[]{:S(2)}, u32[]{:S(2)}) collective-permute-start(f32[8,1,16]{0,2,1:T(8,128)S(1)} %get-tuple-element.314), channel_id=1, source_target_pairs={{8,0},{16,8},{24,16},{32,24},{40,32},{48,40},{56,48},{64,56},{72,6... | collective-permute-start | bytes 1544 | tf_op jit(solution)/shard_map/ppermute | solution.py:21
  308.3 5.3 collective-permute-start.45
  313.7 7.0 %collective-permute-start.46 = (f32[8,4,1]{0,2,1:T(1,128)S(1)}, f32[8,4,1]{0,2,1:T(1,128)S(1)}, u32[]{:S(2)}, u32[]{:S(2)}) collective-permute-start(f32[8,4,1]{0,2,1:T(1,128)S(1)} %get-tuple-element.265), channel_id=1, source_target_pairs={{1,0},{2,1},{3,2},{4,3},{5,4},{6,5},{7,6},{9,8},{10,9},{11,10},{12... | collective-permute-start | bytes 392 | tf_op jit(solution)/shard_map/ppermute | solution.py:21
  315.6 5.8 collective-permute-start.47
  414.4 5.4 collective-permute-start.48
  420.5 15.3 %collective-permute-start.50 = (f32[8,4,1]{0,2,1:T(1,128)S(1)}, f32[8,4,1]{0,2,1:T(1,128)S(1)}, u32[]{:S(2)}, u32[]{:S(2)}) collective-permute-start(f32[8,4,1]{0,2,1:T(1,128)S(1)} %get-tuple-element.263), channel_id=1, source_target_pairs={{1,0},{2,1},{3,2},{4,3},{5,4},{6,5},{7,6},{9,8},{10,9},{11,10},{12... | collective-permute-start | bytes 392 | tf_op jit(solution)/shard_map/ppermute | solution.py:21
  436.8 5.9 %collective-permute-start.52 = (f32[8,1,16]{0,2,1:T(8,128)S(1)}, f32[8,1,16]{0,2,1:T(8,128)S(1)}, u32[]{:S(2)}, u32[]{:S(2)}) collective-permute-start(f32[8,1,16]{0,2,1:T(8,128)S(1)} %get-tuple-element.302), channel_id=1, source_target_pairs={{8,0},{16,8},{24,16},{32,24},{40,32},{48,40},{56,48},{64,56},{72,6... | collective-permute-start | bytes 1544 | tf_op jit(solution)/shard_map/ppermute | solution.py:21
  438.1 5.3 collective-permute-start.53
  443.5 6.7 %collective-permute-start.54 = (f32[8,4,1]{0,2,1:T(1,128)S(1)}, f32[8,4,1]{0,2,1:T(1,128)S(1)}, u32[]{:S(2)}, u32[]{:S(2)}) collective-permute-start(f32[8,4,1]{0,2,1:T(1,128)S(1)} %get-tuple-element.261), channel_id=1, source_target_pairs={{1,0},{2,1},{3,2},{4,3},{5,4},{6,5},{7,6},{9,8},{10,9},{11,10},{12... | collective-permute-start | bytes 392 | tf_op jit(solution)/shard_map/ppermute | solution.py:21
  451.0 5.4 collective-permute-start.57
  459.9 7.3 %collective-permute-start.58 = (f32[8,6,1]{2,0,1:T(8,128)S(1)}, f32[8,6,1]{2,0,1:T(8,128)S(1)}, u32[]{:S(2)}, u32[]{:S(2)}) collective-permute-start(f32[8,6,1]{2,0,1:T(8,128)S(1)} %get-tuple-element.287), channel_id=1, source_target_pairs={{1,0},{2,1},{3,2},{4,3},{5,4},{6,5},{7,6},{9,8},{10,9},{11,10},{12... | collective-permute-start | bytes 584 | tf_op jit(solution)/shard_map/ppermute | solution.py:21
  461.8 6.3 %collective-permute-start.59 = (f32[8,6,1]{2,0,1:T(8,128)S(1)}, f32[8,6,1]{2,0,1:T(8,128)S(1)}, u32[]{:S(2)}, u32[]{:S(2)}) collective-permute-start(f32[8,6,1]{2,0,1:T(8,128)S(1)} %get-tuple-element.288), channel_id=1, source_target_pairs={{0,1},{1,2},{2,3},{3,4},{4,5},{5,6},{6,7},{8,9},{9,10},{10,11},{11... | collective-permute-start | bytes 584 | tf_op jit(solution)/shard_map/ppermute | solution.py:20
  476.7 7.7 %collective-permute-start.62 = (f32[8,6,1]{2,0,1:T(8,128)S(1)}, f32[8,6,1]{2,0,1:T(8,128)S(1)}, u32[]{:S(2)}, u32[]{:S(2)}) collective-permute-start(f32[8,6,1]{2,0,1:T(8,128)S(1)} %get-tuple-element.283), channel_id=1, source_target_pairs={{1,0},{2,1},{3,2},{4,3},{5,4},{6,5},{7,6},{9,8},{10,9},{11,10},{12... | collective-permute-start | bytes 584 | tf_op jit(solution)/shard_map/ppermute | solution.py:21
  478.6 6.6 %collective-permute-start.63 = (f32[8,6,1]{2,0,1:T(8,128)S(1)}, f32[8,6,1]{2,0,1:T(8,128)S(1)}, u32[]{:S(2)}, u32[]{:S(2)}) collective-permute-start(f32[8,6,1]{2,0,1:T(8,128)S(1)} %get-tuple-element.284), channel_id=1, source_target_pairs={{0,1},{1,2},{2,3},{3,4},{4,5},{5,6},{6,7},{8,9},{9,10},{10,11},{11... | collective-permute-start | bytes 584 | tf_op jit(solution)/shard_map/ppermute | solution.py:20
  486.0 5.5 collective-permute-start.65
  494.8 7.6 %collective-permute-start.66 = (f32[8,10,1]{2,0,1:T(8,128)S(1)}, f32[8,10,1]{2,0,1:T(8,128)S(1)}, u32[]{:S(2)}, u32[]{:S(2)}) collective-permute-start(f32[8,10,1]{2,0,1:T(8,128)S(1)} %get-tuple-element.239), channel_id=1, source_target_pairs={{1,0},{2,1},{3,2},{4,3},{5,4},{6,5},{7,6},{9,8},{10,9},{11,10},{12... | collective-permute-start | bytes 968 | tf_op jit(solution)/shard_map/ppermute | solution.py:21
  496.7 6.5 %collective-permute-start.67 = (f32[8,10,1]{2,0,1:T(8,128)S(1)}, f32[8,10,1]{2,0,1:T(8,128)S(1)}, u32[]{:S(2)}, u32[]{:S(2)}) collective-permute-start(f32[8,10,1]{2,0,1:T(8,128)S(1)} %get-tuple-element.240), channel_id=1, source_target_pairs={{0,1},{1,2},{2,3},{3,4},{4,5},{5,6},{6,7},{8,9},{9,10},{10,11},{11... | collective-permute-start | bytes 968 | tf_op jit(solution)/shard_map/ppermute | solution.py:20
  511.6 7.5 %collective-permute-start.70 = (f32[8,10,1]{2,0,1:T(8,128)S(1)}, f32[8,10,1]{2,0,1:T(8,128)S(1)}, u32[]{:S(2)}, u32[]{:S(2)}) collective-permute-start(f32[8,10,1]{2,0,1:T(8,128)S(1)} %get-tuple-element.235), channel_id=1, source_target_pairs={{1,0},{2,1},{3,2},{4,3},{5,4},{6,5},{7,6},{9,8},{10,9},{11,10},{12... | collective-permute-start | bytes 968 | tf_op jit(solution)/shard_map/ppermute | solution.py:21
  513.5 6.6 %collective-permute-start.71 = (f32[8,10,1]{2,0,1:T(8,128)S(1)}, f32[8,10,1]{2,0,1:T(8,128)S(1)}, u32[]{:S(2)}, u32[]{:S(2)}) collective-permute-start(f32[8,10,1]{2,0,1:T(8,128)S(1)} %get-tuple-element.236), channel_id=1, source_target_pairs={{0,1},{1,2},{2,3},{3,4},{4,5},{5,6},{6,7},{8,9},{9,10},{10,11},{11... | collective-permute-start | bytes 968 | tf_op jit(solution)/shard_map/ppermute | solution.py:20
  520.8 7.0 %collective-permute-start.73 = (f32[8,1,128]{2,1,0:T(1,128)S(1)}, f32[8,1,128]{2,1,0:T(1,128)S(1)}, u32[]{:S(2)}, u32[]{:S(2)}) collective-permute-start(f32[8,1,128]{2,1,0:T(1,128)S(1)} %get-tuple-element.182), channel_id=1, source_target_pairs={{0,8},{8,16},{16,24},{24,32},{32,40},{40,48},{48,56},{56,64},{64,7... | collective-permute-start | bytes 12296 | tf_op jit(solution)/shard_map/ppermute | solution.py:20
  531.1 7.4 %collective-permute-start.74 = (f32[8,18,1]{2,0,1:T(8,128)S(1)}, f32[8,18,1]{2,0,1:T(8,128)S(1)}, u32[]{:S(2)}, u32[]{:S(2)}) collective-permute-start(f32[8,18,1]{2,0,1:T(8,128)S(1)} %get-tuple-element.155), channel_id=1, source_target_pairs={{1,0},{2,1},{3,2},{4,3},{5,4},{6,5},{7,6},{9,8},{10,9},{11,10},{12... | collective-permute-start | bytes 1736 | tf_op jit(solution)/shard_map/ppermute | solution.py:21
  533.0 6.8 %collective-permute-start.75 = (f32[8,18,1]{2,0,1:T(8,128)S(1)}, f32[8,18,1]{2,0,1:T(8,128)S(1)}, u32[]{:S(2)}, u32[]{:S(2)}) collective-permute-start(f32[8,18,1]{2,0,1:T(8,128)S(1)} %get-tuple-element.156), channel_id=1, source_target_pairs={{0,1},{1,2},{2,3},{3,4},{4,5},{5,6},{6,7},{8,9},{9,10},{10,11},{11... | collective-permute-start | bytes 1736 | tf_op jit(solution)/shard_map/ppermute | solution.py:20
  540.0 6.2 %collective-permute-start.77 = (f32[8,1,128]{2,1,0:T(1,128)S(1)}, f32[8,1,128]{2,1,0:T(1,128)S(1)}, u32[]{:S(2)}, u32[]{:S(2)}) collective-permute-start(f32[8,1,128]{2,1,0:T(1,128)S(1)} %get-tuple-element.176), channel_id=1, source_target_pairs={{0,8},{8,16},{16,24},{24,32},{32,40},{40,48},{48,56},{56,64},{64,7... | collective-permute-start | bytes 12296 | tf_op jit(solution)/shard_map/ppermute | solution.py:20
  549.6 7.5 %collective-permute-start.78 = (f32[8,18,1]{2,0,1:T(8,128)S(1)}, f32[8,18,1]{2,0,1:T(8,128)S(1)}, u32[]{:S(2)}, u32[]{:S(2)}) collective-permute-start(f32[8,18,1]{2,0,1:T(8,128)S(1)} %get-tuple-element.151), channel_id=1, source_target_pairs={{1,0},{2,1},{3,2},{4,3},{5,4},{6,5},{7,6},{9,8},{10,9},{11,10},{12... | collective-permute-start | bytes 1736 | tf_op jit(solution)/shard_map/ppermute | solution.py:21
  551.5 6.8 %collective-permute-start.79 = (f32[8,18,1]{2,0,1:T(8,128)S(1)}, f32[8,18,1]{2,0,1:T(8,128)S(1)}, u32[]{:S(2)}, u32[]{:S(2)}) collective-permute-start(f32[8,18,1]{2,0,1:T(8,128)S(1)} %get-tuple-element.152), channel_id=1, source_target_pairs={{0,1},{1,2},{2,3},{3,4},{4,5},{5,6},{6,7},{8,9},{9,10},{10,11},{11... | collective-permute-start | bytes 1736 | tf_op jit(solution)/shard_map/ppermute | solution.py:20
  558.6 5.1 collective-permute-start.81
  567.1 7.5 %collective-permute-start.82 = (f32[8,18,1]{2,0,1:T(8,128)S(1)}, f32[8,18,1]{2,0,1:T(8,128)S(1)}, u32[]{:S(2)}, u32[]{:S(2)}) collective-permute-start(f32[8,18,1]{2,0,1:T(8,128)S(1)} %get-tuple-element.147), channel_id=1, source_target_pairs={{1,0},{2,1},{3,2},{4,3},{5,4},{6,5},{7,6},{9,8},{10,9},{11,10},{12... | collective-permute-start | bytes 1736 | tf_op jit(solution)/shard_map/ppermute | solution.py:21
  569.0 6.8 %collective-permute-start.83 = (f32[8,18,1]{2,0,1:T(8,128)S(1)}, f32[8,18,1]{2,0,1:T(8,128)S(1)}, u32[]{:S(2)}, u32[]{:S(2)}) collective-permute-start(f32[8,18,1]{2,0,1:T(8,128)S(1)} %get-tuple-element.148), channel_id=1, source_target_pairs={{0,1},{1,2},{2,3},{3,4},{4,5},{5,6},{6,7},{8,9},{9,10},{10,11},{11... | collective-permute-start | bytes 1736 | tf_op jit(solution)/shard_map/ppermute | solution.py:20
  (60 other events, 2703.6 us)
where the time goes:
time: 583 us; the launch traced here: 577 us
  starting transfers between devices  281 us (48%)
  blocking collectives  121 us (21%)
  waiting for transfers between devices  62.2 us (11%)
  local copies, waits for them, and re-layouts  57.7 us (10%)
  other arithmetic  30.9 us (5%)
  between operations  23.7 us (4%)
    ppermute x42, starting transfers between devices, extended(): before = lax.ppermute(last, axis, up)  189 us
    ppermute x42, starting transfers between devices, extended(): after = lax.ppermute(leading, axis, down)  92.7 us
    all_gather x2, blocking collectives, collect(): return lax.all_gather(gathered, 'gx', axis=2, tiled=True)  91.7 us
    ppermute x42, waiting for transfers between devices, extended(): after = lax.ppermute(leading, axis, down)  41.1 us
    all_gather x2, blocking collectives, collect(): gathered = lax.all_gather(stacked, 'gy', axis=3, tiled=True)  29.1 us
    ppermute x42, waiting for transfers between devices, extended(): before = lax.ppermute(last, axis, up)  21.1 us
    unnamed x97, local copies, waits for them, and re-layouts  16.9 us
    reduce_sum x15, other arithmetic, local_total(): return jnp.sum(values)  12.6 us
  transfers between devices with their start and end apart: 84, of which 42 were waited for; matrix products, arithmetic and copies ran while one was open for 12% of the time, Pallas kernels for 0%

commit v1 on v0

v1 whole, which is shorter than its diff:
```python
import jax
import jax.numpy as jnp
from jax import lax
from jax.experimental import pallas as pl
from jax.experimental.pallas import tpu as pltpu
from jax.sharding import PartitionSpec as P

MESH = pl.DeviceIdType.MESH
NGX, NGY = 32, 8
OMEGA = 0.8
SPAN = 0.25**4
SWEEPS = 8
F32 = jnp.float32

LOW = (8, 4, 8, 4)
ROWS = (32, 16, 20, 10)


def lanes():
    return lax.broadcasted_iota(jnp.int32, (8, 128), 1)


def swap(x):
    return jnp.concatenate([x[:, 1:2], x[:, 0:1]], axis=1)


def north(x, step):
    turned = pltpu.roll(x, 128 - step, 3)
    return jnp.where(lanes() >= 128 - step, swap(turned), turned)


def south(x, step):
    turned = pltpu.roll(x, step, 3)
    return jnp.where(lanes() < step, swap(turned), turned)


def upper(x):
    return pltpu.roll(x, 7, x.ndim - 2)


def lower(x):
    return pltpu.roll(x, 1, x.ndim - 2)


def operate(v, cx, cy, cz, step):
    fx = cx * (v[:-1] - v[1:])
    mid = v[1:-1]
    fy = cy * (mid - north(mid, step))
    fz = cz * (mid - upper(mid))
    return (fx[1:] - fx[:-1]) + (fy - south(fy, step)) + (fz - lower(fz))


def pair_mean(total, step):
    axis = total.ndim - 1
    low = (lanes() // step) % 2 == 0
    other = jnp.where(low, pltpu.roll(total, 128 - step, axis), pltpu.roll(total, step, axis))
    return 0.25 * (total + other)


def coarsen(x, step):
    rows = x.shape[0]
    y = x.reshape((rows // 2, 2) + x.shape[1:])
    return pair_mean(y[:, 0] + y[:, 1], step)


def pick(x, index):
    return jnp.take_along_axis(x, index, axis=1)


def kernel(f_ref, m_ref, s_ref, q_ref,
           e0, kr, kl, rkl, rkr, rm2, rf2, ma, mb, fa, fb, rv3, rv1, v4, c4,
           f1, f2, f3, w0, w1, w2, w3, cx0, cx1, cx2, cx3, cy0, cy1, cy2, cy3, cz0, cz1, cz2, cz3,
           va0, va1, va2, va3, vb0, vb1, vb2, vb3,
           tiles, lines, ssem, r1_sem, recv):
    gx, gy = lax.axis_index("gx"), lax.axis_index("gy")
    xc, zc = gx // 8, gx % 8
    yc, cc = gy // 2, gy % 2
    CX, CY, CZ, W = (cx0, cx1, cx2, cx3), (cy0, cy1, cy2, cy3), (cz0, cz1, cz2, cz3), (w0, w1, w2, w3)
    VA, VB = (va0, va1, va2, va3), (vb0, vb1, vb2, vb3)
    lane = lanes()
    sub = lax.broadcasted_iota(jnp.int32, (8, 128), 0)

    def beside(dx, dy):
        return ((gx + dx + NGX) % NGX, (gy + dy + NGY) % NGY)

    wide = [(dx, dy) for dx in (-2, -1, 0, 1, 2) for dy in (-1, 0, 1) if (dx, dy) != (0, 0)]
    column = [(xc * 8 + (zc + dz) % 8, yc * 2 + (cc + dc) % 2) for dz in range(8) for dc in range(2) if (dz, dc) != (0, 0)]
    plane = [(((xc + dx) % 4) * 8 + zc, ((yc + dy) % 4) * 2 + cc) for dx in range(4) for dy in range(4) if (dx, dy) != (0, 0)]

    barrier = pltpu.get_barrier_semaphore()
    everyone = [beside(dx, dy) for dx, dy in wide] + column + plane
    for target in everyone:
        pl.semaphore_signal(barrier, inc=1, device_id=target, device_id_type=MESH)

    def send(src, dst, sem, to, out):
        copy = pltpu.make_async_remote_copy(
            src_ref=src, dst_ref=dst, send_sem=ssem.at[out], recv_sem=sem, device_id=to, device_id_type=MESH)
        copy.start()
        return copy

    def pieces(kind, count, sem):
        ref = kind.at[pl.ds(0, count)]
        pltpu.make_async_copy(ref, ref, sem).wait()

    for row in range(16):
        for arr in range(4):
            if arr == 1:
                tile = f_ref[pl.ds(row, 8, 16), :]
            else:
                tile = m_ref[pl.ds((arr - 1 if arr else 0) * 128 + row, 8, 16), :]
            e0[arr, 8 + row, 0] = tile
    for k in range(4):
        right, left = jnp.zeros((8, 128), F32), jnp.zeros((8, 128), F32)
        for g in range(16):
            turned = pltpu.roll(e0[g % 4, 8 + 4 * k + g // 4, 0], (8 * g + 8) % 128, 1)
            right = jnp.where(lane // 8 == g, turned, right)
            left = jnp.where(lane // 8 == (g + 1) % 16, turned, left)
        kr[k] = right
        kl[k] = left

    def spread_row(tile):
        turned = pick(tile, 16 * (lane % 8))
        return jnp.sum(jnp.where(sub == lane // 16, turned, 0.0), axis=0, keepdims=True)

    for comp in range(3):
        arr = (0, 2, 3)[comp]
        m1 = coarsen(e0[arr, 8:24, 0], 1)
        m2 = coarsen(m1, 2)
        m3 = coarsen(m2, 4)
        m4 = coarsen(m3, 8)
        part = lane % 4
        rm2[7, comp] = jnp.where(part == 0, m2[0], jnp.where(part == 1, m2[1], jnp.where(part == 2, m2[2], m2[3])))
        ma[cc, comp, pl.ds(zc, 1)] = spread_row(m4[0])

    pl.semaphore_wait(barrier, len(everyone))

    sends = []
    east, west = beside(1, 0), beside(-1, 0)
    rest = pl.ds(1, 3)
    sends.append(send(e0.at[0, pl.ds(16, 8), 0], e0.at[0, pl.ds(0, 8), 0], r1_sem.at[0], east, 0))
    sends.append(send(e0.at[0, pl.ds(8, 8), 0], e0.at[0, pl.ds(24, 8), 0], r1_sem.at[1], west, 1))
    sends.append(send(e0.at[rest, pl.ds(18, 6), 0], e0.at[rest, pl.ds(2, 6), 0], r1_sem.at[2], east, 2))
    sends.append(send(e0.at[rest, pl.ds(8, 6), 0], e0.at[rest, pl.ds(24, 6), 0], r1_sem.at[3], west, 3))
    for side, (packed, into) in enumerate(((kr, rkl), (kl, rkr))):
        dy = 1 - 2 * side
        for n, (dx, a, b, c) in enumerate(((1, 2, 2, 0), (-1, 0, 2, 6), (0, 0, 4, 2))):
            slot = 4 + 3 * side + n
            sends.append(send(packed.at[pl.ds(a, b)], into.at[pl.ds(c, b)], r1_sem.at[slot], beside(dx, dy), slot))
    for dx, dy in wide:
        send(rm2.at[7], rm2.at[7 - dx * 3 - dy], recv.at[0], beside(dx, dy), 10)
    for target in column:
        mine = ma.at[cc, pl.ds(0, 3), pl.ds(zc, 1)]
        send(mine, mine, recv.at[1], target, 11)
    for copy in sends:
        copy.wait_recv()

    even = (lane // 8) % 2 == 0
    for k in range(8):
        me = jnp.where(even, rkl[k], rkr[k])
        mo = jnp.where(even, rkr[k], rkl[k])
        for g in range(16):
            e0[g % 4, 4 * k + g // 4, 1] = pltpu.roll(me if g % 2 == 0 else mo, (120 - 8 * g) % 128, 1)

    has_left, has_right = gy > 0, gy < NGY - 1

    def side_mask(reach):
        inside = jnp.logical_or(jnp.logical_and(lane < reach, has_right), jnp.logical_and(lane >= 128 - reach, has_left))
        return inside.astype(F32)

    mask0, mask2 = side_mask(8), side_mask(64)

    def row_inside(level, row):
        own = 16 >> level
        if row < 0:
            need = -(row // own)
            return (gx >= need).astype(F32)
        if row >= own:
            return (gx + row // own <= NGX - 1).astype(F32)
        return None

    def masked(tile, level, row, part):
        side = mask0 if level < 2 else mask2
        scale = row_inside(level, row)
        if part == 1:
            tile = tile * side
        return tile if scale is None else tile * scale

    for arr in (0, 2, 3):
        for row in range(-8 if arr == 0 else -6, 24 if arr == 0 else 22):
            for part in range(2):
                if part == 1 or row < 0 or row >= 16:
                    e0[arr, row + 8, part] = masked(e0[arr, row + 8, part], 0, row, part)

    def coefficients(level, mx, my, mz, lo, hi):
        low, step = LOW[level], 1 << level
        half, spans = 0.5 * 0.25**level, 0.5 * SPAN
        for a in range(lo, hi, 4):
            b = min(a + 4, hi)
            x = mx(a - 1, b + 1)
            cx = half * (x[:-1] + x[1:])
            y = my(a, b)
            cy = half * (y + north(y, step))
            z = mz(a, b)
            cz = spans * (z + upper(z))
            CX[level][a - 1 + low:b + low] = cx
            CY[level][a + low:b + low] = cy
            CZ[level][a + low:b + low] = cz
            diag = cx[:-1] + cx[1:] + cy + south(cy, step) + cz + lower(cz)
            w = OMEGA / diag
            for row in range(a, b):
                for part in range(2):
                    tile = w[row - a, part]
                    side = mask0 if level < 2 else mask2
                    scale = row_inside(level, row)
                    if part == 1:
                        tile = jnp.where(side > 0, tile, 0.0)
                    if scale is not None:
                        tile = jnp.where(scale > 0, tile, 0.0)
                    W[level][row + low, part] = tile

    def field(level, source, target, lo, hi, f_of, relax, chunk=4):
        low, step = LOW[level], 1 << level
        for a in range(lo, hi, chunk):
            b = min(a + chunk, hi)
            v = source[a - 1 + low:b + 1 + low]
            left = f_of(a, b) - operate(
                v, CX[level][a - 1 + low:b + low], CY[level][a + low:b + low], CZ[level][a + low:b + low], step)
            target(a, b, v[1:-1] + W[level][a + low:b + low] * left if relax else left)

    def into(ref, level):
        def store(a, b, value):
            ref[a + LOW[level]:b + LOW[level]] = value
        return store

    def into_coarse(ref, level):
        def store(a, b, value):
            ref[a // 2 + LOW[level + 1]:b // 2 + LOW[level + 1]] = coarsen(value, 1 << level)
        return store

    def rows_of(ref, level):
        return lambda a, b: ref[a + LOW[level]:b + LOW[level]]

    def start(level, f_of, lo, hi):
        low = LOW[level]
        for a in range(lo, hi, 4):
            b = min(a + 4, hi)
            VA[level][a + low:b + low] = W[level][a + low:b + low] * f_of(a, b)

    def arr0(arr):
        return lambda a, b: e0[arr, a + 8:b + 8]

    coefficients(0, arr0(0), arr0(2), arr0(3), -6, 22)
    start(0, arr0(1), -6, 22)
    field(0, va0, into(vb0, 0), -5, 21, arr0(1), True)
    field(0, vb0, into_coarse(f1, 0), -4, 20, arr0(1), False)

    def coarse0(arr):
        return lambda a, b: coarsen(e0[arr, 2 * a + 8:2 * b + 8], 1)

    coefficients(1, coarse0(0), coarse0(2), coarse0(3), -3, 11)
    start(1, rows_of(f1, 1), -2, 10)
    field(1, va1, into(vb1, 1), -1, 9, rows_of(f1, 1), True)
    own2 = []

    def keep(a, b, value):
        own2.append(coarsen(value[:, 0], 2))

    field(1, vb1, keep, 0, 8, rows_of(f1, 1), False)
    part = lane % 4
    rf2[7] = jnp.where(part == 0, own2[0][0], jnp.where(part == 1, own2[0][1], jnp.where(part == 2, own2[1][0], own2[1][1])))
    for dx, dy in wide:
        send(rf2.at[7], rf2.at[7 - dx * 3 - dy], recv.at[2], beside(dx, dy), 12)

    pieces(tiles, 42, recv.at[0])
    pieces(lines, 45, recv.at[1])
    own4 = [jnp.where((lane // 8) % 2 == 0, ma[0, comp], ma[1, comp]) for comp in range(3)]
    for comp in range(3):
        mb[xc, yc, comp] = own4[comp]
    for target in plane:
        send(mb.at[xc, yc], mb.at[xc, yc], recv.at[3], target, 13)

    quads = [(lane // 4) * 4 + j for j in range(4)]

    def rows2(of, a, b):
        out = []
        for row in range(a, b):
            block = (row // 4 + 2) * 3
            main = of(block + 1)
            side = jnp.where(lane < 64, of(block + 2), of(block))
            out.append(jnp.stack([pick(main, quads[row % 4]), pick(side, quads[row % 4])]))
        return jnp.stack(out)

    def metric2(comp):
        def rows(a, b):
            got = rows2(lambda slot: rm2[slot, comp], a, b)
            return jnp.stack([jnp.stack([masked(got[n, p], 2, a + n, p) for p in range(2)]) for n in range(b - a)])
        return rows

    def metric3(comp):
        return lambda a, b: coarsen(metric2(comp)(2 * a, 2 * b), 4)

    coefficients(2, metric2(0), metric2(1), metric2(2), -7, 11)
    coefficients(3, metric3(0), metric3(1), metric3(2), -3, 5)

    pieces(tiles, 14, recv.at[2])
    for a in range(-6, 10, 4):
        f2[a + 8:a + 12] = rows2(lambda slot: rf2[slot], a, a + 4)
    start(2, rows_of(f2, 2), -6, 10)
    field(2, va2, into(vb2, 2), -5, 9, rows_of(f2, 2), True)
    field(2, vb2, into_coarse(f3, 2), -4, 8, rows_of(f2, 2), False)
    start(3, rows_of(f3, 3), -2, 4)
    field(3, va3, into(vb3, 3), -1, 3, rows_of(f3, 3), True)
    own4f = []

    def keep4(a, b, value):
        own4f.append(coarsen(value[:, 0], 8))

    field(3, vb3, keep4, 0, 2, rows_of(f3, 3), False)
    fa[cc, pl.ds(zc, 1)] = spread_row(own4f[0][0])
    for target in column:
        mine = fa.at[cc, pl.ds(zc, 1)]
        send(mine, mine, recv.at[4], target, 14)

    pieces(tiles, 45, recv.at[3])
    lane16 = lane % 16
    four = 0.5 * 0.25**4

    def next_x(v):
        turned = upper(v)
        return jnp.where(sub == 7, jnp.concatenate([turned[1:], turned[:1]], axis=0), turned)

    def last_x(v):
        turned = lower(v)
        return jnp.where(sub == 0, jnp.concatenate([turned[3:], turned[:3]], axis=0), turned)

    def next_y(v):
        far = pltpu.roll(v, 15, 3)
        return jnp.where(lane16 == 15, jnp.concatenate([far[:, 1:], far[:, :1]], axis=1), pltpu.roll(v, 127, 3))

    def last_y(v):
        far = pltpu.roll(v, 113, 3)
        return jnp.where(lane16 == 0, jnp.concatenate([far[:, 3:], far[:, :3]], axis=1), pltpu.roll(v, 1, 3))

    def next_z(v):
        return pltpu.roll(v, 112, 3)

    def last_z(v):
        return pltpu.roll(v, 16, 3)

    def blank(x, axis, where, cond):
        pieces = []
        for n in range(4):
            piece = lax.slice_in_dim(x, n, n + 1, axis=axis)
            pieces.append(jnp.where(cond, 0.0, piece) if n == where else piece)
        return jnp.concatenate(pieces, axis=axis)

    mx, my, mz = mb[:, :, 0], mb[:, :, 1], mb[:, :, 2]
    mxe, mxw = blank(next_x(mx), 0, 3, sub == 7), blank(last_x(mx), 0, 0, sub == 0)
    myn, mys = blank(next_y(my), 1, 3, lane16 == 15), blank(last_y(my), 1, 0, lane16 == 0)
    ce, cw, cn, cs = four * (mx + mxe), four * (mx + mxw), four * (my + myn), four * (my + mys)
    cu, cl = four * (mz + next_z(mz)), four * (mz + last_z(mz))
    c4[6] = ce + cw + cn + cs + cu + cl
    c4[0] = blank(ce, 0, 3, sub == 7)
    c4[1] = blank(cw, 0, 0, sub == 0)
    c4[2] = blank(cn, 1, 3, lane16 == 15)
    c4[3] = blank(cs, 1, 0, lane16 == 0)
    c4[4] = cu
    c4[5] = cl

    pieces(lines, 15, recv.at[4])
    fb[xc, yc] = jnp.where((lane // 8) % 2 == 0, fa[0], fa[1])
    for target in plane:
        send(fb.at[xc, yc], fb.at[xc, yc], recv.at[5], target, 15)

    rv3[7] = jnp.where(part == 0, vb3[4, 0], jnp.where(part == 1, vb3[5, 0], jnp.where(part == 2, f3[4, 0], f3[5, 0])))
    for dx, dy in wide:
        send(rv3.at[7], rv3.at[7 - dx * 3 - dy], recv.at[6], beside(dx, dy), 16)
    for row in range(8):
        rv1[1, 4 + row] = jnp.where(lane % 2 == 0, vb1[4 + row, 0], f1[4 + row, 0])
    for dx in (-1, 0, 1):
        for dy in (-1, 0, 1):
            if (dx, dy) != (0, 0):
                a, b, c = ((4, 4, 12), (4, 8, 4), (8, 4, 0))[dx + 1]
                send(rv1.at[1, pl.ds(a, b)], rv1.at[1 - dy, pl.ds(c, b)], recv.at[7], beside(dx, dy), 17)

    pieces(tiles, 15, recv.at[5])

    def total(x):
        tile = jnp.sum(x, axis=(0, 1))
        return jnp.sum(jnp.sum(tile, axis=0, keepdims=True), axis=1, keepdims=True)

    def image_of(p):
        out = c4[6] * p - c4[0] * next_x(p) - c4[1] * last_x(p)
        out = out - c4[2] * next_y(p) - c4[3] * last_y(p)
        return out - c4[4] * next_z(p) - c4[5] * last_z(p)

    r = fb[...]
    p = r
    v = jnp.zeros_like(r)
    rr = total(r * r)
    for sweep in range(SWEEPS):
        q = image_of(p)
        alpha = rr / total(p * q)
        v = v + alpha * p
        if sweep + 1 < SWEEPS:
            r = r - alpha * q
            new = total(r * r)
            p = r + (new / rr) * p
            rr = new
    v4[...] = v

    main_index = sub * 16 + cc * 8 + lane // 16
    side_index = sub * 16 + (cc * 8 + 8 + lane // 16) % 16
    other_y = jnp.clip(yc + 2 * cc - 1, 0, 3)
    near = jnp.logical_xor(lane < 64, cc == 1)
    pieces(tiles, 14, recv.at[6])
    octs = [(lane // 8) * 8 + j for j in range(4)]
    for d in range(-2, 3):
        x = jnp.clip(gx + d, 0, NGX - 1)
        here = jnp.broadcast_to(v4[x // 8, yc, pl.ds(x % 8, 1)], (8, 128))
        there = jnp.broadcast_to(v4[x // 8, other_y, pl.ds(x % 8, 1)], (8, 128))
        main = pick(here, main_index)
        side = jnp.where(near, pick(here, side_index), pick(there, side_index)) * mask2
        block = (d + 2) * 3
        packed = (rv3[block + 1], jnp.where(lane < 64, rv3[block + 2], rv3[block]))
        inside = row_inside(3, 2 * d)
        for j in range(2):
            row = 2 * d + j
            for p_no in range(2):
                value = pick(packed[p_no], octs[j])
                if p_no == 1:
                    value = value * mask2
                value = value + (main if p_no == 0 else side)
                va3[row + 4, p_no] = value if inside is None else value * inside
                if -3 <= row < 5:
                    f3[row + 4, p_no] = pick(packed[p_no], octs[2 + j])
    field(3, va3, into(vb3, 3), -3, 5, rows_of(f3, 3), True)
    field(3, vb3, into(va3, 3), -2, 4, rows_of(f3, 3), True)

    def refined(ref, level, a, b):
        x = ref[a + LOW[level]:b + LOW[level]]
        return jnp.stack([x, x], axis=1).reshape((2 * (b - a),) + x.shape[1:])

    def correct(level, a, b):
        low = LOW[level]
        for n in range(a, b, 4):
            m = min(n + 4, b)
            VA[level][n + low:m + low] = VB[level][n + low:m + low] + refined(VA[level + 1], level + 1, n // 2, m // 2)

    correct(2, -4, 8)
    field(2, va2, into(vb2, 2), -3, 7, rows_of(f2, 2), True)
    field(2, vb2, into(va2, 2), -2, 6, rows_of(f2, 2), True)

    pieces(tiles, 40, recv.at[7])
    evens, odds = (lane // 2) * 2, (lane // 2) * 2 + 1
    for row in range(-4, 12):
        inside = row_inside(1, row)
        if inside is not None:
            value = pick(rv1[1, row + 4], evens)
            vb1[row + 4, 0] = value * inside
            f1[row + 4, 0] = pick(rv1[1, row + 4], odds)
        packed = jnp.where(lane < 64, rv1[2, row + 4], rv1[0, row + 4])
        value = pick(packed, evens) * mask0
        vb1[row + 4, 1] = value if inside is None else value * inside
        f1[row + 4, 1] = pick(packed, odds)
    correct(1, -4, 12)
    field(1, va1, into(vb1, 1), -3, 11, rows_of(f1, 1), True)
    field(1, vb1, into(va1, 1), -2, 10, rows_of(f1, 1), True)

    for a in range(-2, 9):
        lo = -3 if a == -2 else 2 * a
        hi = 2 * a + 2
        add = va1[a + 4]
        for row in range(lo, hi):
            va0[row + 8] = vb0[row + 8] + add
    va0[18 + 8] = vb0[18 + 8] + va1[9 + 4]
    field(0, va0, into(vb0, 0), -2, 18, arr0(1), True)

    def out_stream(a, b, value):
        va0[a + 8:b + 8] = value
        for row in range(max(a, 0), min(b, 16)):
            s_ref[pl.ds(row, 8, 16), :] = value[row - a, 0]

    def out_residual(a, b, value):
        for row in range(a, b):
            q_ref[pl.ds(row, 8, 16), :] = value[row - a, 0]

    field(0, vb0, out_stream, -1, 17, arr0(1), True)
    field(0, va0, out_residual, 0, 16, arr0(1), False)

    for copy in sends:
        copy.wait_send()
    for group, (kind, count) in enumerate(
            ((tiles, 42), (lines, 45), (tiles, 14), (tiles, 45), (lines, 15), (tiles, 15), (tiles, 14), (tiles, 40))):
        pieces(kind, count, ssem.at[10 + group])


def level_scratch():
    shapes = []
    for level in range(4):
        shapes.append(pltpu.VMEM((ROWS[level], 2, 8, 128), F32))
    return shapes


def on_device(vorticity, metric):
    depth, rows, columns = vorticity.shape
    tile = (8, 128)
    scratch = [
        pltpu.VMEM((4, 32, 2) + tile, F32),
        pltpu.VMEM((4,) + tile, F32), pltpu.VMEM((4,) + tile, F32),
        pltpu.VMEM((8,) + tile, F32), pltpu.VMEM((8,) + tile, F32),
        pltpu.VMEM((15, 3) + tile, F32), pltpu.VMEM((15,) + tile, F32),
        pltpu.VMEM((2, 3) + tile, F32), pltpu.VMEM((4, 4, 3) + tile, F32),
        pltpu.VMEM((2,) + tile, F32), pltpu.VMEM((4, 4) + tile, F32),
        pltpu.VMEM((15,) + tile, F32), pltpu.VMEM((3, 16) + tile, F32),
        pltpu.VMEM((4, 4) + tile, F32), pltpu.VMEM((7, 4, 4) + tile, F32),
    ]
    scratch += level_scratch()[1:]
    for _ in range(6):
        scratch += level_scratch()
    scratch += [pltpu.VMEM((45,) + tile, F32), pltpu.VMEM((45, 1, 128), F32)]
    scratch += [pltpu.SemaphoreType.DMA((18,)), pltpu.SemaphoreType.DMA((10,)), pltpu.SemaphoreType.DMA((8,))]
    flat = jax.ShapeDtypeStruct((depth * rows, columns), F32)
    vmem = pl.BlockSpec(memory_space=pltpu.VMEM)
    stream, residual = pl.pallas_call(
        kernel,
        out_shape=(flat, flat),
        in_specs=[vmem, vmem],
        out_specs=(vmem, vmem),
        scratch_shapes=scratch,
        compiler_params=pltpu.CompilerParams(collective_id=0, has_side_effects=True, vmem_limit_bytes=48 * 1024 * 1024),
    )(vorticity.reshape(depth * rows, columns), metric.reshape(3 * depth * rows, columns))
    return stream.reshape(vorticity.shape), residual.reshape(vorticity.shape)


def solution(mesh):
    return jax.shard_map(
        on_device,
        mesh=mesh,
        in_specs=(P(None, "gx", "gy"), P(None, None, "gx", "gy")),
        out_specs=(P(None, "gx", "gy"), P(None, "gx", "gy")),
        check_vma=False,
    )
```

time: 583 us -> 42.3 us (0.07); the launches traced: 577 us -> 42.2 us
  starting transfers between devices: 281 us -> 0 us
  blocking collectives: 121 us -> 0 us
  waiting for transfers between devices: 62.2 us -> 0 us
  local copies, waits for them, and re-layouts: 57.7 us -> 3.02 us
  Pallas kernels: 0 us -> 38.5 us
  other arithmetic: 30.9 us -> 0 us
  between operations: 23.7 us -> 0.65 us
    ppermute x84 -> x0, starting transfers between devices: 281 us -> none  [the longest x42 189 us: extended(): before = lax.ppermute(last, axis, up)]
    all_gather x4 -> x0, blocking collectives: 121 us -> none  [the longest x2 91.7 us: collect(): return lax.all_gather(gathered, 'gx', axis=2, tiled=True)]
    ppermute x84 -> x0, waiting for transfers between devices: 62.2 us -> none  [the longest x42 41.1 us: extended(): after = lax.ppermute(leading, axis, down)]
    pallas_call x0 -> x1, Pallas kernels: none -> 38.5 us  [on_device(): pl.pallas_call(kernel, out_shape=(flat, flat), in_specs=[vmem, vmem], out...]
    slice x109 -> x0, local copies, waits for them, and re-layouts: 33.5 us -> none  [the longest x2 8.83 us: face_coeffs(): c_upper = 0.5 * (m_z + jnp.roll(m_z, -1, 0)) * span_scale]
    reduce_sum x25 -> x0, other arithmetic: 18.5 us -> none  [the longest x15 12.6 us: local_total(): return jnp.sum(values)]
    unnamed x97 -> x6, local copies, waits for them, and re-layouts: 16.9 us -> 3.02 us
    concatenate x33 -> x0, other arithmetic: 6.94 us -> none  [extended(): x = jnp.concatenate([before, x, after], axis=dim)]
  transfers between devices with their start and end apart: 84 -> 0, of which waited for: 42 -> 0; matrix products, arithmetic and copies ran while one was open for 12% -> 0% of each run, Pallas kernels for 0% -> 0%
where the time goes in v1:
time: 42.3 us; the launch traced here: 42.2 us
  Pallas kernels  38.5 us (91%)
  local copies, waits for them, and re-layouts  3.02 us (7%)
  between operations  0.65 us (2%)
    pallas_call x1, Pallas kernels, on_device(): pl.pallas_call(kernel, out_shape=(flat, flat), in_specs=[vmem, vmem], out...  38.5 us
    unnamed x6, local copies, waits for them, and re-layouts  3.02 us

profile of v1, /device:TPU:1, one launch (start us, length us, event | category | flops | bytes accessed | tf_op | source)
XLA Modules:
  0.0 42.2 jit_solution(1274239131569993850)
XLA Ops:
  0.6 0.0 copy-start
  0.6 0.9 %copy-done = f32[3,8,16,128]{3,2,1,0:T(8,128)S(1)} copy-done((f32[3,8,16,128]{3,2,1,0:T(8,128)S(1)}, f32[3,8,16,128]{3,2,1,0:T(8,128)}, u32[]{:S(2)}) %copy-start) | copy-done | bytes 196632
  1.6 0.0 copy-start.1
  1.6 0.8 %copy-done.1 = f32[8,16,128]{2,1,0:T(8,128)S(1)} copy-done((f32[8,16,128]{2,1,0:T(8,128)S(1)}, f32[8,16,128]{2,1,0:T(8,128)}, u32[]{:S(2)}) %copy-start.1) | copy-done | bytes 65560
  2.4 38.5 %shard_map.41 = (f32[128,128]{1,0:T(8,128)S(1)}, f32[128,128]{1,0:T(8,128)S(1)}) custom-call(f32[128,128]{1,0:T(8,128)S(1)} %bitcast.7, f32[384,128]{1,0:T(8,128)S(1)} %bitcast.4), custom_call_target="tpu_custom_call" | custom-call | tf_op jit(solution)/shard_map/pallas_call | solution.py:525
  40.9 0.6 %copy.6 = f32[8,16,128]{2,1,0:T(8,128)} copy(f32[8,16,128]{2,1,0:T(8,128)S(1)} %bitcast.6) | data formatting | bytes 131072
  41.5 0.6 %copy.7 = f32[8,16,128]{2,1,0:T(8,128)} copy(f32[8,16,128]{2,1,0:T(8,128)S(1)} %bitcast.5) | data formatting | bytes 131072
Async XLA Ops:
  0.6 0.9 %copy-start = (f32[3,8,16,128]{3,2,1,0:T(8,128)S(1)}, f32[3,8,16,128]{3,2,1,0:T(8,128)}, u32[]{:S(2)}) copy-start(f32[3,8,16,128]{3,2,1,0:T(8,128)} %param.3) | copy-start | bytes 589828
  1.6 0.8 %copy-start.1 = (f32[8,16,128]{2,1,0:T(8,128)S(1)}, f32[8,16,128]{2,1,0:T(8,128)}, u32[]{:S(2)}) copy-start(f32[8,16,128]{2,1,0:T(8,128)} %param.2) | copy-start | bytes 196612

commit v2 on v1

--- a/solution.py
+++ b/solution.py
@@ -50,17 +50,20 @@
     return (fx[1:] - fx[:-1]) + (fy - south(fy, step)) + (fz - lower(fz))
 
 
-def pair_mean(total, step):
-    axis = total.ndim - 1
-    low = (lanes() // step) % 2 == 0
-    other = jnp.where(low, pltpu.roll(total, 128 - step, axis), pltpu.roll(total, step, axis))
-    return 0.25 * (total + other)
-
-
-def coarsen(x, step):
-    rows = x.shape[0]
-    y = x.reshape((rows // 2, 2) + x.shape[1:])
-    return pair_mean(y[:, 0] + y[:, 1], step)
+def coarsen_field(x, step):
+    y = x.reshape((x.shape[0] // 2, 2) + x.shape[1:])
+    both, axis = y[:, 0] + y[:, 1], x.ndim - 1
+    other = jnp.where((lanes() & step) == 0, pltpu.roll(both, 128 - step, axis), pltpu.roll(both, step, axis))
+    return 0.25 * (both + other)
+
+
+def moved(x, matrix):
+    first = x.astype(jnp.bfloat16)
+    rest = x - first.astype(F32)
+    second = rest.astype(jnp.bfloat16)
+    third = (rest - second.astype(F32)).astype(jnp.bfloat16)
+    terms = [jnp.dot(term, matrix, preferred_element_type=F32) for term in (first, second, third)]
+    return terms[0] + (terms[1] + terms[2])
 
 
 def pick(x, index):
@@ -68,17 +71,18 @@
 
 
 def kernel(f_ref, m_ref, s_ref, q_ref,
-           e0, kr, kl, rkl, rkr, rm2, rf2, ma, mb, fa, fb, rv3, rv1, v4, c4,
+           e0, m1, pairs, f_in, m_in, in_sem, kr, kl, rkl, rkr, rm2, rf2, ma, mb, fa, fb, rv3, rv1, v4, c4,
            f1, f2, f3, w0, w1, w2, w3, cx0, cx1, cx2, cx3, cy0, cy1, cy2, cy3, cz0, cz1, cz2, cz3,
            va0, va1, va2, va3, vb0, vb1, vb2, vb3,
            tiles, lines, ssem, r1_sem, recv):
     gx, gy = lax.axis_index("gx"), lax.axis_index("gy")
-    xc, zc = gx // 8, gx % 8
-    yc, cc = gy // 2, gy % 2
+    xc, zc = gx >> 3, gx & 7
+    yc, cc = gy >> 1, gy & 1
     CX, CY, CZ, W = (cx0, cx1, cx2, cx3), (cy0, cy1, cy2, cy3), (cz0, cz1, cz2, cz3), (w0, w1, w2, w3)
     VA, VB = (va0, va1, va2, va3), (vb0, vb1, vb2, vb3)
     lane = lanes()
     sub = lax.broadcasted_iota(jnp.int32, (8, 128), 0)
+    slot = lane >> 3
 
     def beside(dx, dy):
         return ((gx + dx + NGX) % NGX, (gy + dy + NGY) % NGY)
@@ -86,6 +90,13 @@
     wide = [(dx, dy) for dx in (-2, -1, 0, 1, 2) for dy in (-1, 0, 1) if (dx, dy) != (0, 0)]
     column = [(xc * 8 + (zc + dz) % 8, yc * 2 + (cc + dc) % 2) for dz in range(8) for dc in range(2) if (dz, dc) != (0, 0)]
     plane = [(((xc + dx) % 4) * 8 + zc, ((yc + dy) % 4) * 2 + cc) for dx in range(4) for dy in range(4) if (dx, dy) != (0, 0)]
+
+    def pair_mean(total, step):
+        return moved(total.reshape(-1, 128), pairs[step.bit_length() - 1]).reshape(total.shape)
+
+    def coarsen(x, step):
+        y = x.reshape((x.shape[0] // 2, 2) + x.shape[1:])
+        return pair_mean(y[:, 0] + y[:, 1], step)
 
     barrier = pltpu.get_barrier_semaphore()
     everyone = [beside(dx, dy) for dx, dy in wide] + column + plane
@@ -102,35 +113,37 @@
         ref = kind.at[pl.ds(0, count)]
         pltpu.make_async_copy(ref, ref, sem).wait()
 
+    source = lax.broadcasted_iota(jnp.int32, (128, 128), 0)
+    goal = lax.broadcasted_iota(jnp.int32, (128, 128), 1)
+
+    def matrix_of(condition, value=1.0):
+        return jnp.where(condition, value, 0.0).astype(jnp.bfloat16)
+
+    loads = [pltpu.make_async_copy(m_ref, m_in, in_sem.at[0]), pltpu.make_async_copy(f_ref, f_in, in_sem.at[1])]
+    for copy in loads:
+        copy.start()
+    for copy in loads:
+        copy.wait()
+
     for row in range(16):
         for arr in range(4):
             if arr == 1:
-                tile = f_ref[pl.ds(row, 8, 16), :]
+                tile = f_in[pl.ds(row, 8, 16), :]
             else:
-                tile = m_ref[pl.ds((arr - 1 if arr else 0) * 128 + row, 8, 16), :]
+                tile = m_in[pl.ds((arr - 1 if arr else 0) * 128 + row, 8, 16), :]
             e0[arr, 8 + row, 0] = tile
     for k in range(4):
         right, left = jnp.zeros((8, 128), F32), jnp.zeros((8, 128), F32)
         for g in range(16):
             turned = pltpu.roll(e0[g % 4, 8 + 4 * k + g // 4, 0], (8 * g + 8) % 128, 1)
-            right = jnp.where(lane // 8 == g, turned, right)
-            left = jnp.where(lane // 8 == (g + 1) % 16, turned, left)
+            right = jnp.where(slot == g, turned, right)
+            left = jnp.where(slot == (g + 1) % 16, turned, left)
         kr[k] = right
         kl[k] = left
 
     def spread_row(tile):
-        turned = pick(tile, 16 * (lane % 8))
-        return jnp.sum(jnp.where(sub == lane // 16, turned, 0.0), axis=0, keepdims=True)
-
-    for comp in range(3):
-        arr = (0, 2, 3)[comp]
-        m1 = coarsen(e0[arr, 8:24, 0], 1)
-        m2 = coarsen(m1, 2)
-        m3 = coarsen(m2, 4)
-        m4 = coarsen(m3, 8)
-        part = lane % 4
-        rm2[7, comp] = jnp.where(part == 0, m2[0], jnp.where(part == 1, m2[1], jnp.where(part == 2, m2[2], m2[3])))
-        ma[cc, comp, pl.ds(zc, 1)] = spread_row(m4[0])
+        turned = pick(tile, 16 * (lane & 7))
+        return jnp.sum(jnp.where(sub == (lane >> 4), turned, 0.0), axis=0, keepdims=True)
 
     pl.semaphore_wait(barrier, len(everyone))
 
@@ -144,8 +157,19 @@
     for side, (packed, into) in enumerate(((kr, rkl), (kl, rkr))):
         dy = 1 - 2 * side
         for n, (dx, a, b, c) in enumerate(((1, 2, 2, 0), (-1, 0, 2, 6), (0, 0, 4, 2))):
-            slot = 4 + 3 * side + n
-            sends.append(send(packed.at[pl.ds(a, b)], into.at[pl.ds(c, b)], r1_sem.at[slot], beside(dx, dy), slot))
+            at = 4 + 3 * side + n
+            sends.append(send(packed.at[pl.ds(a, b)], into.at[pl.ds(c, b)], r1_sem.at[at], beside(dx, dy), at))
+    for n in range(4):
+        pairs[n] = matrix_of(jnp.logical_or(source == goal, source == (goal ^ (1 << n))), 0.25)
+    for comp in range(3):
+        arr = (0, 2, 3)[comp]
+        m2 = coarsen(coarsen(e0[arr, 8:24, 0], 1), 2)
+        m3 = coarsen(m2, 4)
+        m4 = coarsen(m3, 8)
+        part = lane & 3
+        rm2[7, comp] = jnp.where(part == 0, m2[0], jnp.where(part == 1, m2[1], jnp.where(part == 2, m2[2], m2[3])))
+        ma[cc, comp, pl.ds(zc, 1)] = spread_row(m4[0])
+
     for dx, dy in wide:
         send(rm2.at[7], rm2.at[7 - dx * 3 - dy], recv.at[0], beside(dx, dy), 10)
     for target in column:
@@ -154,7 +178,7 @@
     for copy in sends:
         copy.wait_recv()
 
-    even = (lane // 8) % 2 == 0
+    even = (lane & 8) == 0
     for k in range(8):
         me = jnp.where(even, rkl[k], rkr[k])
         mo = jnp.where(even, rkr[k], rkl[k])
@@ -234,7 +258,7 @@
 
     def into_coarse(ref, level):
         def store(a, b, value):
-            ref[a // 2 + LOW[level + 1]:b // 2 + LOW[level + 1]] = coarsen(value, 1 << level)
+            ref[a // 2 + LOW[level + 1]:b // 2 + LOW[level + 1]] = coarsen_field(value, 1 << level)
         return store
 
     def rows_of(ref, level):
@@ -254,32 +278,36 @@
     field(0, va0, into(vb0, 0), -5, 21, arr0(1), True)
     field(0, vb0, into_coarse(f1, 0), -4, 20, arr0(1), False)
 
-    def coarse0(arr):
-        return lambda a, b: coarsen(e0[arr, 2 * a + 8:2 * b + 8], 1)
-
-    coefficients(1, coarse0(0), coarse0(2), coarse0(3), -3, 11)
+    for comp, arr in enumerate((0, 2, 3)):
+        lo, hi = (-4, 12) if arr == 0 else (-3, 11)
+        m1[comp, lo + 4:hi + 4] = coarsen(e0[arr, 2 * lo + 8:2 * hi + 8], 1)
+
+    def coarse1(comp):
+        return lambda a, b: m1[comp, a + 4:b + 4]
+
+    coefficients(1, coarse1(0), coarse1(1), coarse1(2), -3, 11)
     start(1, rows_of(f1, 1), -2, 10)
     field(1, va1, into(vb1, 1), -1, 9, rows_of(f1, 1), True)
     own2 = []
 
     def keep(a, b, value):
-        own2.append(coarsen(value[:, 0], 2))
+        own2.append(coarsen_field(value[:, 0], 2))
 
     field(1, vb1, keep, 0, 8, rows_of(f1, 1), False)
-    part = lane % 4
+    part = lane & 3
     rf2[7] = jnp.where(part == 0, own2[0][0], jnp.where(part == 1, own2[0][1], jnp.where(part == 2, own2[1][0], own2[1][1])))
     for dx, dy in wide:
         send(rf2.at[7], rf2.at[7 - dx * 3 - dy], recv.at[2], beside(dx, dy), 12)
 
     pieces(tiles, 42, recv.at[0])
     pieces(lines, 45, recv.at[1])
-    own4 = [jnp.where((lane // 8) % 2 == 0, ma[0, comp], ma[1, comp]) for comp in range(3)]
+    own4 = [jnp.where((lane & 8) == 0, ma[0, comp], ma[1, comp]) for comp in range(3)]
     for comp in range(3):
         mb[xc, yc, comp] = own4[comp]
     for target in plane:
         send(mb.at[xc, yc], mb.at[xc, yc], recv.at[3], target, 13)
 
-    quads = [(lane // 4) * 4 + j for j in range(4)]
+    quads = [(lane & ~3) + j for j in range(4)]
 
     def rows2(of, a, b):
         out = []
@@ -313,7 +341,7 @@
     own4f = []
 
     def keep4(a, b, value):
-        own4f.append(coarsen(value[:, 0], 8))
+        own4f.append(coarsen_field(value[:, 0], 8))
 
     field(3, vb3, keep4, 0, 2, rows_of(f3, 3), False)
     fa[cc, pl.ds(zc, 1)] = spread_row(own4f[0][0])
@@ -322,7 +350,7 @@
         send(mine, mine, recv.at[4], target, 14)
 
     pieces(tiles, 45, recv.at[3])
-    lane16 = lane % 16
+    lane16 = lane & 15
     four = 0.5 * 0.25**4
 
     def next_x(v):
@@ -368,7 +396,7 @@
     c4[5] = cl
 
     pieces(lines, 15, recv.at[4])
-    fb[xc, yc] = jnp.where((lane // 8) % 2 == 0, fa[0], fa[1])
+    fb[xc, yc] = jnp.where((lane & 8) == 0, fa[0], fa[1])
     for target in plane:
         send(fb.at[xc, yc], fb.at[xc, yc], recv.at[5], target, 15)
 
@@ -376,7 +404,7 @@
     for dx, dy in wide:
         send(rv3.at[7], rv3.at[7 - dx * 3 - dy], recv.at[6], beside(dx, dy), 16)
     for row in range(8):
-        rv1[1, 4 + row] = jnp.where(lane % 2 == 0, vb1[4 + row, 0], f1[4 + row, 0])
+        rv1[1, 4 + row] = jnp.where((lane & 1) == 0, vb1[4 + row, 0], f1[4 + row, 0])
     for dx in (-1, 0, 1):
         for dy in (-1, 0, 1):
             if (dx, dy) != (0, 0):
@@ -395,30 +423,34 @@
         return out - c4[4] * next_z(p) - c4[5] * last_z(p)
 
     r = fb[...]
-    p = r
-    v = jnp.zeros_like(r)
-    rr = total(r * r)
+    p = q = v = rr = alpha = None
     for sweep in range(SWEEPS):
-        q = image_of(p)
-        alpha = rr / total(p * q)
-        v = v + alpha * p
+        image = image_of(r)
+        new, power = total(r * r), total(r * image)
+        if sweep == 0:
+            p, q, alpha = r, image, new / power
+            v = alpha * p
+        else:
+            beta = new / rr
+            alpha = new / (power - beta * new / alpha)
+            p = r + beta * p
+            q = image + beta * q
+            v = v + alpha * p
+        rr = new
         if sweep + 1 < SWEEPS:
             r = r - alpha * q
-            new = total(r * r)
-            p = r + (new / rr) * p
-            rr = new
     v4[...] = v
 
-    main_index = sub * 16 + cc * 8 + lane // 16
-    side_index = sub * 16 + (cc * 8 + 8 + lane // 16) % 16
+    main_index = sub * 16 + cc * 8 + (lane >> 4)
+    side_index = sub * 16 + ((cc * 8 + 8 + (lane >> 4)) & 15)
     other_y = jnp.clip(yc + 2 * cc - 1, 0, 3)
     near = jnp.logical_xor(lane < 64, cc == 1)
     pieces(tiles, 14, recv.at[6])
-    octs = [(lane // 8) * 8 + j for j in range(4)]
+    octs = [(lane & ~7) + j for j in range(4)]
     for d in range(-2, 3):
         x = jnp.clip(gx + d, 0, NGX - 1)
-        here = jnp.broadcast_to(v4[x // 8, yc, pl.ds(x % 8, 1)], (8, 128))
-        there = jnp.broadcast_to(v4[x // 8, other_y, pl.ds(x % 8, 1)], (8, 128))
+        here = jnp.broadcast_to(v4[x >> 3, yc, pl.ds(x & 7, 1)], (8, 128))
+        there = jnp.broadcast_to(v4[x >> 3, other_y, pl.ds(x & 7, 1)], (8, 128))
         main = pick(here, main_index)
         side = jnp.where(near, pick(here, side_index), pick(there, side_index)) * mask2
         block = (d + 2) * 3
@@ -452,7 +484,7 @@
     field(2, vb2, into(va2, 2), -2, 6, rows_of(f2, 2), True)
 
     pieces(tiles, 40, recv.at[7])
-    evens, odds = (lane // 2) * 2, (lane // 2) * 2 + 1
+    evens, odds = lane & ~1, lane | 1
     for row in range(-4, 12):
         inside = row_inside(1, row)
         if inside is not None:
@@ -506,7 +538,10 @@
     depth, rows, columns = vorticity.shape
     tile = (8, 128)
     scratch = [
-        pltpu.VMEM((4, 32, 2) + tile, F32),
+        pltpu.VMEM((4, 32, 2) + tile, F32), pltpu.VMEM((3, 16, 2) + tile, F32),
+        pltpu.VMEM((4, 128, 128), jnp.bfloat16),
+        pltpu.VMEM((depth * rows, columns), F32), pltpu.VMEM((3 * depth * rows, columns), F32),
+        pltpu.SemaphoreType.DMA((2,)),
         pltpu.VMEM((4,) + tile, F32), pltpu.VMEM((4,) + tile, F32),
         pltpu.VMEM((8,) + tile, F32), pltpu.VMEM((8,) + tile, F32),
         pltpu.VMEM((15, 3) + tile, F32), pltpu.VMEM((15,) + tile, F32),
@@ -525,7 +560,7 @@
     stream, residual = pl.pallas_call(
         kernel,
         out_shape=(flat, flat),
-        in_specs=[vmem, vmem],
+        in_specs=[pl.BlockSpec(memory_space=pl.ANY)] * 2,
         out_specs=(vmem, vmem),
         scratch_shapes=scratch,
         compiler_params=pltpu.CompilerParams(collective_id=0, has_side_effects=True, vmem_limit_bytes=48 * 1024 * 1024),

time: 42.3 us -> 40.9 us (0.967)
  Pallas kernels: 38.5 us -> 37.1 us
    pallas_call x1, Pallas kernels: 38.5 us -> 37.1 us  [on_device(): pl.pallas_call(kernel, out_shape=(flat, flat), in_specs=[pl.BlockSpec(mem...]
where the time goes in v2:
time: 40.9 us; the launch traced here: 40.8 us
  Pallas kernels  37.1 us (91%)
  local copies, waits for them, and re-layouts  3.02 us (7%)
  between operations  0.65 us (2%)
    pallas_call x1, Pallas kernels, on_device(): pl.pallas_call(kernel, out_shape=(flat, flat), in_specs=[pl.BlockSpec(mem...  37.1 us
    unnamed x6, local copies, waits for them, and re-layouts  3.02 us

profile of v2, /device:TPU:1, one launch (start us, length us, event | category | flops | bytes accessed | tf_op | source)
XLA Modules:
  0.0 40.8 jit_solution(1041217948280977799)
XLA Ops:
  0.6 0.0 copy-start
  0.6 0.9 %copy-done = f32[3,8,16,128]{3,2,1,0:T(8,128)S(1)} copy-done((f32[3,8,16,128]{3,2,1,0:T(8,128)S(1)}, f32[3,8,16,128]{3,2,1,0:T(8,128)}, u32[]{:S(2)}) %copy-start) | copy-done | bytes 196632
  1.6 0.0 copy-start.1
  1.6 0.8 %copy-done.1 = f32[8,16,128]{2,1,0:T(8,128)S(1)} copy-done((f32[8,16,128]{2,1,0:T(8,128)S(1)}, f32[8,16,128]{2,1,0:T(8,128)}, u32[]{:S(2)}) %copy-start.1) | copy-done | bytes 65560
  2.4 37.1 %shard_map.41 = (f32[128,128]{1,0:T(8,128)S(1)}, f32[128,128]{1,0:T(8,128)S(1)}) custom-call(f32[128,128]{1,0:T(8,128)S(1)} %bitcast.7, f32[384,128]{1,0:T(8,128)S(1)} %bitcast.4), custom_call_target="tpu_custom_call" | custom-call | tf_op jit(solution)/shard_map/pallas_call | solution.py:560
  39.5 0.6 %copy.6 = f32[8,16,128]{2,1,0:T(8,128)} copy(f32[8,16,128]{2,1,0:T(8,128)S(1)} %bitcast.6) | data formatting | bytes 131072
  40.2 0.6 %copy.7 = f32[8,16,128]{2,1,0:T(8,128)} copy(f32[8,16,128]{2,1,0:T(8,128)S(1)} %bitcast.5) | data formatting | bytes 131072
Async XLA Ops:
  0.6 0.9 %copy-start = (f32[3,8,16,128]{3,2,1,0:T(8,128)S(1)}, f32[3,8,16,128]{3,2,1,0:T(8,128)}, u32[]{:S(2)}) copy-start(f32[3,8,16,128]{3,2,1,0:T(8,128)} %param.3) | copy-start | bytes 589828
  1.6 0.8 %copy-start.1 = (f32[8,16,128]{2,1,0:T(8,128)S(1)}, f32[8,16,128]{2,1,0:T(8,128)}, u32[]{:S(2)}) copy-start(f32[8,16,128]{2,1,0:T(8,128)} %param.2) | copy-start | bytes 196612

commit v3 on v2

--- a/solution.py
+++ b/solution.py
@@ -141,9 +141,11 @@
         kr[k] = right
         kl[k] = left
 
+    turn = yc + 4 * (xc >> 1)
+
     def spread_row(tile):
         turned = pick(tile, 16 * (lane & 7))
-        return jnp.sum(jnp.where(sub == (lane >> 4), turned, 0.0), axis=0, keepdims=True)
+        return jnp.sum(jnp.where(sub == (((lane >> 4) - turn) & 7), turned, 0.0), axis=0, keepdims=True)
 
     pl.semaphore_wait(barrier, len(everyone))
 
@@ -300,13 +302,6 @@
         send(rf2.at[7], rf2.at[7 - dx * 3 - dy], recv.at[2], beside(dx, dy), 12)
 
     pieces(tiles, 42, recv.at[0])
-    pieces(lines, 45, recv.at[1])
-    own4 = [jnp.where((lane & 8) == 0, ma[0, comp], ma[1, comp]) for comp in range(3)]
-    for comp in range(3):
-        mb[xc, yc, comp] = own4[comp]
-    for target in plane:
-        send(mb.at[xc, yc], mb.at[xc, yc], recv.at[3], target, 13)
-
     quads = [(lane & ~3) + j for j in range(4)]
 
     def rows2(of, a, b):
@@ -331,6 +326,13 @@
     coefficients(3, metric3(0), metric3(1), metric3(2), -3, 5)
 
     pieces(tiles, 14, recv.at[2])
+    pieces(lines, 45, recv.at[1])
+    own4 = [jnp.where((lane & 8) == 0, ma[0, comp], ma[1, comp]) for comp in range(3)]
+    for comp in range(3):
+        mb[xc, yc, comp] = own4[comp]
+    for target in plane:
+        send(mb.at[xc, yc], mb.at[xc, yc], recv.at[3], target, 13)
+
     for a in range(-6, 10, 4):
         f2[a + 8:a + 12] = rows2(lambda slot: rf2[slot], a, a + 4)
     start(2, rows_of(f2, 2), -6, 10)
@@ -348,52 +350,6 @@
     for target in column:
         mine = fa.at[cc, pl.ds(zc, 1)]
         send(mine, mine, recv.at[4], target, 14)
-
-    pieces(tiles, 45, recv.at[3])
-    lane16 = lane & 15
-    four = 0.5 * 0.25**4
-
-    def next_x(v):
-        turned = upper(v)
-        return jnp.where(sub == 7, jnp.concatenate([turned[1:], turned[:1]], axis=0), turned)
-
-    def last_x(v):
-        turned = lower(v)
-        return jnp.where(sub == 0, jnp.concatenate([turned[3:], turned[:3]], axis=0), turned)
-
-    def next_y(v):
-        far = pltpu.roll(v, 15, 3)
-        return jnp.where(lane16 == 15, jnp.concatenate([far[:, 1:], far[:, :1]], axis=1), pltpu.roll(v, 127, 3))
-
-    def last_y(v):
-        far = pltpu.roll(v, 113, 3)
-        return jnp.where(lane16 == 0, jnp.concatenate([far[:, 3:], far[:, :3]], axis=1), pltpu.roll(v, 1, 3))
-
-    def next_z(v):
-        return pltpu.roll(v, 112, 3)
-
-    def last_z(v):
-        return pltpu.roll(v, 16, 3)
-
-    def blank(x, axis, where, cond):
-        pieces = []
-        for n in range(4):
-            piece = lax.slice_in_dim(x, n, n + 1, axis=axis)
-            pieces.append(jnp.where(cond, 0.0, piece) if n == where else piece)
-        return jnp.concatenate(pieces, axis=axis)
-
-    mx, my, mz = mb[:, :, 0], mb[:, :, 1], mb[:, :, 2]
-    mxe, mxw = blank(next_x(mx), 0, 3, sub == 7), blank(last_x(mx), 0, 0, sub == 0)
-    myn, mys = blank(next_y(my), 1, 3, lane16 == 15), blank(last_y(my), 1, 0, lane16 == 0)
-    ce, cw, cn, cs = four * (mx + mxe), four * (mx + mxw), four * (my + myn), four * (my + mys)
-    cu, cl = four * (mz + next_z(mz)), four * (mz + last_z(mz))
-    c4[6] = ce + cw + cn + cs + cu + cl
-    c4[0] = blank(ce, 0, 3, sub == 7)
-    c4[1] = blank(cw, 0, 0, sub == 0)
-    c4[2] = blank(cn, 1, 3, lane16 == 15)
-    c4[3] = blank(cs, 1, 0, lane16 == 0)
-    c4[4] = cu
-    c4[5] = cl
 
     pieces(lines, 15, recv.at[4])
     fb[xc, yc] = jnp.where((lane & 8) == 0, fa[0], fa[1])
@@ -411,18 +367,60 @@
                 a, b, c = ((4, 4, 12), (4, 8, 4), (8, 4, 0))[dx + 1]
                 send(rv1.at[1, pl.ds(a, b)], rv1.at[1 - dy, pl.ds(c, b)], recv.at[7], beside(dx, dy), 17)
 
+    pieces(tiles, 45, recv.at[3])
+    four = 0.5 * 0.25**4
+    column_y = lane & 63
+    first_half = lane < 64
+    whose = ((lane >> 4) - sub) & 7
+    unturn = (lane + 16 * sub) & 127
+
+    def whole(row_of):
+        out = []
+        for r in range(16):
+            mixed = None
+            for k in range(8):
+                row = jnp.broadcast_to(row_of((r >> 3) + 2 * (k >> 2), k & 3, r & 7), (8, 128))
+                mixed = row if k == 0 else jnp.where(whose == k, row, mixed)
+            out.append(pick(mixed, unturn))
+        return jnp.stack(out)
+
+    def next_x(v):
+        return jnp.concatenate([v[1:], jnp.where(first_half, pltpu.roll(v[0:1], 64, 2), 0.0)], axis=0)
+
+    def last_x(v):
+        return jnp.concatenate([jnp.where(first_half, 0.0, pltpu.roll(v[15:16], 64, 2)), v[:-1]], axis=0)
+
+    def next_y(v):
+        return pltpu.roll(v, 127, 2)
+
+    def last_y(v):
+        return pltpu.roll(v, 1, 2)
+
+    mx, my, mz = [whole(lambda a, b, c, comp=comp: mb[a, b, comp, c:c + 1]) for comp in range(3)]
+    ce, cw = four * (mx + next_x(mx)), four * (mx + last_x(mx))
+    cn = four * (my + jnp.where(column_y == 63, 0.0, next_y(my)))
+    cs = four * (my + jnp.where(column_y == 0, 0.0, last_y(my)))
+    cu, cl = four * (mz + upper(mz)), four * (mz + lower(mz))
+    c4[0] = ce
+    c4[1] = cw
+    c4[2] = jnp.where(column_y == 63, 0.0, cn)
+    c4[3] = jnp.where(column_y == 0, 0.0, cs)
+    c4[4] = cu
+    c4[5] = cl
+    c4[6] = ce + cw + cn + cs + cu + cl
+
     pieces(tiles, 15, recv.at[5])
 
     def total(x):
-        tile = jnp.sum(x, axis=(0, 1))
+        tile = jnp.sum(x, axis=0)
         return jnp.sum(jnp.sum(tile, axis=0, keepdims=True), axis=1, keepdims=True)
 
     def image_of(p):
         out = c4[6] * p - c4[0] * next_x(p) - c4[1] * last_x(p)
         out = out - c4[2] * next_y(p) - c4[3] * last_y(p)
-        return out - c4[4] * next_z(p) - c4[5] * last_z(p)
-
-    r = fb[...]
+        return out - c4[4] * upper(p) - c4[5] * lower(p)
+
+    r = whole(lambda a, b, c: fb[a, b, c:c + 1])
     p = q = v = rr = alpha = None
     for sweep in range(SWEEPS):
         image = image_of(r)
@@ -441,18 +439,14 @@
             r = r - alpha * q
     v4[...] = v
 
-    main_index = sub * 16 + cc * 8 + (lane >> 4)
-    side_index = sub * 16 + ((cc * 8 + 8 + (lane >> 4)) & 15)
-    other_y = jnp.clip(yc + 2 * cc - 1, 0, 3)
-    near = jnp.logical_xor(lane < 64, cc == 1)
     pieces(tiles, 14, recv.at[6])
     octs = [(lane & ~7) + j for j in range(4)]
     for d in range(-2, 3):
         x = jnp.clip(gx + d, 0, NGX - 1)
-        here = jnp.broadcast_to(v4[x >> 3, yc, pl.ds(x & 7, 1)], (8, 128))
-        there = jnp.broadcast_to(v4[x >> 3, other_y, pl.ds(x & 7, 1)], (8, 128))
-        main = pick(here, main_index)
-        side = jnp.where(near, pick(here, side_index), pick(there, side_index)) * mask2
+        tile = v4[x & 15]
+        half = (x >> 4) * 64
+        main = pick(tile, half + gy * 8 + (lane >> 4))
+        side = pick(tile, half + ((gy * 8 + jnp.where(first_half, 8, -8) + (lane >> 4)) & 63)) * mask2
         block = (d + 2) * 3
         packed = (rv3[block + 1], jnp.where(lane < 64, rv3[block + 2], rv3[block]))
         inside = row_inside(3, 2 * d)
@@ -548,7 +542,7 @@
         pltpu.VMEM((2, 3) + tile, F32), pltpu.VMEM((4, 4, 3) + tile, F32),
         pltpu.VMEM((2,) + tile, F32), pltpu.VMEM((4, 4) + tile, F32),
         pltpu.VMEM((15,) + tile, F32), pltpu.VMEM((3, 16) + tile, F32),
-        pltpu.VMEM((4, 4) + tile, F32), pltpu.VMEM((7, 4, 4) + tile, F32),
+        pltpu.VMEM((16,) + tile, F32), pltpu.VMEM((7, 16) + tile, F32),
     ]
     scratch += level_scratch()[1:]
     for _ in range(6):

time: 40.9 us -> 40.1 us (0.980)
  Pallas kernels: 37.1 us -> 36.3 us
    pallas_call x1, Pallas kernels: 37.1 us -> 36.3 us  [on_device(): pl.pallas_call(kernel, out_shape=(flat, flat), in_specs=[pl.BlockSpec(mem...]
where the time goes in v3:
time: 40.1 us; the launch traced here: 39.9 us
  Pallas kernels  36.3 us (91%)
  local copies, waits for them, and re-layouts  3.02 us (8%)
  between operations  0.65 us (2%)
    pallas_call x1, Pallas kernels, on_device(): pl.pallas_call(kernel, out_shape=(flat, flat), in_specs=[pl.BlockSpec(mem...  36.3 us
    unnamed x6, local copies, waits for them, and re-layouts  3.02 us

profile of v3, /device:TPU:1, one launch (start us, length us, event | category | flops | bytes accessed | tf_op | source)
XLA Modules:
  0.0 39.9 jit_solution(3539511055828957245)
XLA Ops:
  0.6 0.0 copy-start
  0.6 0.9 %copy-done = f32[3,8,16,128]{3,2,1,0:T(8,128)S(1)} copy-done((f32[3,8,16,128]{3,2,1,0:T(8,128)S(1)}, f32[3,8,16,128]{3,2,1,0:T(8,128)}, u32[]{:S(2)}) %copy-start) | copy-done | bytes 196632
  1.6 0.0 copy-start.1
  1.6 0.8 %copy-done.1 = f32[8,16,128]{2,1,0:T(8,128)S(1)} copy-done((f32[8,16,128]{2,1,0:T(8,128)S(1)}, f32[8,16,128]{2,1,0:T(8,128)}, u32[]{:S(2)}) %copy-start.1) | copy-done | bytes 65560
  2.4 36.3 %shard_map.41 = (f32[128,128]{1,0:T(8,128)S(1)}, f32[128,128]{1,0:T(8,128)S(1)}) custom-call(f32[128,128]{1,0:T(8,128)S(1)} %bitcast.7, f32[384,128]{1,0:T(8,128)S(1)} %bitcast.4), custom_call_target="tpu_custom_call" | custom-call | tf_op jit(solution)/shard_map/pallas_call | solution.py:554
  38.7 0.6 %copy.6 = f32[8,16,128]{2,1,0:T(8,128)} copy(f32[8,16,128]{2,1,0:T(8,128)S(1)} %bitcast.6) | data formatting | bytes 131072
  39.3 0.6 %copy.7 = f32[8,16,128]{2,1,0:T(8,128)} copy(f32[8,16,128]{2,1,0:T(8,128)S(1)} %bitcast.5) | data formatting | bytes 131072
Async XLA Ops:
  0.6 0.9 %copy-start = (f32[3,8,16,128]{3,2,1,0:T(8,128)S(1)}, f32[3,8,16,128]{3,2,1,0:T(8,128)}, u32[]{:S(2)}) copy-start(f32[3,8,16,128]{3,2,1,0:T(8,128)} %param.3) | copy-start | bytes 589828
  1.6 0.8 %copy-start.1 = (f32[8,16,128]{2,1,0:T(8,128)S(1)}, f32[8,16,128]{2,1,0:T(8,128)}, u32[]{:S(2)}) copy-start(f32[8,16,128]{2,1,0:T(8,128)} %param.2) | copy-start | bytes 196612

commit v4 on v3

--- a/solution.py
+++ b/solution.py
@@ -351,14 +351,14 @@
         mine = fa.at[cc, pl.ds(zc, 1)]
         send(mine, mine, recv.at[4], target, 14)
 
+    rv3[7] = jnp.where(part == 0, vb3[4, 0], jnp.where(part == 1, vb3[5, 0], jnp.where(part == 2, f3[4, 0], f3[5, 0])))
+    for dx, dy in wide:
+        send(rv3.at[7], rv3.at[7 - dx * 3 - dy], recv.at[6], beside(dx, dy), 16)
     pieces(lines, 15, recv.at[4])
     fb[xc, yc] = jnp.where((lane & 8) == 0, fa[0], fa[1])
     for target in plane:
         send(fb.at[xc, yc], fb.at[xc, yc], recv.at[5], target, 15)
 
-    rv3[7] = jnp.where(part == 0, vb3[4, 0], jnp.where(part == 1, vb3[5, 0], jnp.where(part == 2, f3[4, 0], f3[5, 0])))
-    for dx, dy in wide:
-        send(rv3.at[7], rv3.at[7 - dx * 3 - dy], recv.at[6], beside(dx, dy), 16)
     for row in range(8):
         rv1[1, 4 + row] = jnp.where((lane & 1) == 0, vb1[4 + row, 0], f1[4 + row, 0])
     for dx in (-1, 0, 1):
@@ -409,6 +409,21 @@
     c4[5] = cl
     c4[6] = ce + cw + cn + cs + cu + cl
 
+    pieces(tiles, 14, recv.at[6])
+    octs = [(lane & ~7) + j for j in range(4)]
+    for d in range(-2, 3):
+        block = (d + 2) * 3
+        packed = (rv3[block + 1], jnp.where(first_half, rv3[block + 2], rv3[block]))
+        inside = row_inside(3, 2 * d)
+        for j in range(2):
+            row = 2 * d + j
+            for p_no in range(2):
+                value = pick(packed[p_no], octs[j])
+                if p_no == 1:
+                    value = value * mask2
+                va3[row + 4, p_no] = value if inside is None else value * inside
+                if -3 <= row < 5:
+                    f3[row + 4, p_no] = pick(packed[p_no], octs[2 + j])
     pieces(tiles, 15, recv.at[5])
 
     def total(x):
@@ -439,27 +454,18 @@
             r = r - alpha * q
     v4[...] = v
 
-    pieces(tiles, 14, recv.at[6])
-    octs = [(lane & ~7) + j for j in range(4)]
     for d in range(-2, 3):
         x = jnp.clip(gx + d, 0, NGX - 1)
         tile = v4[x & 15]
         half = (x >> 4) * 64
         main = pick(tile, half + gy * 8 + (lane >> 4))
         side = pick(tile, half + ((gy * 8 + jnp.where(first_half, 8, -8) + (lane >> 4)) & 63)) * mask2
-        block = (d + 2) * 3
-        packed = (rv3[block + 1], jnp.where(lane < 64, rv3[block + 2], rv3[block]))
         inside = row_inside(3, 2 * d)
-        for j in range(2):
-            row = 2 * d + j
-            for p_no in range(2):
-                value = pick(packed[p_no], octs[j])
-                if p_no == 1:
-                    value = value * mask2
-                value = value + (main if p_no == 0 else side)
-                va3[row + 4, p_no] = value if inside is None else value * inside
-                if -3 <= row < 5:
-                    f3[row + 4, p_no] = pick(packed[p_no], octs[2 + j])
+        if inside is not None:
+            main, side = main * inside, side * inside
+        for row in (2 * d, 2 * d + 1):
+            va3[row + 4, 0] = va3[row + 4, 0] + main
+            va3[row + 4, 1] = va3[row + 4, 1] + side
     field(3, va3, into(vb3, 3), -3, 5, rows_of(f3, 3), True)
     field(3, vb3, into(va3, 3), -2, 4, rows_of(f3, 3), True)
 

time: 40.1 us -> 39.9 us (level)
  no operation moved by 1% of the time
where the time goes in v4:
time: 39.9 us; the launch traced here: 39.8 us
  Pallas kernels  36.1 us (90%)
  local copies, waits for them, and re-layouts  3.02 us (8%)
  between operations  0.65 us (2%)
    pallas_call x1, Pallas kernels, on_device(): pl.pallas_call(kernel, out_shape=(flat, flat), in_specs=[pl.BlockSpec(mem...  36.1 us
    unnamed x6, local copies, waits for them, and re-layouts  3.02 us

profile of v4, /device:TPU:1, one launch (start us, length us, event | category | flops | bytes accessed | tf_op | source)
XLA Modules:
  0.0 39.8 jit_solution(17355813474524740564)
XLA Ops:
  0.6 0.0 copy-start
  0.6 0.9 %copy-done = f32[3,8,16,128]{3,2,1,0:T(8,128)S(1)} copy-done((f32[3,8,16,128]{3,2,1,0:T(8,128)S(1)}, f32[3,8,16,128]{3,2,1,0:T(8,128)}, u32[]{:S(2)}) %copy-start) | copy-done | bytes 196632
  1.6 0.0 copy-start.1
  1.6 0.8 %copy-done.1 = f32[8,16,128]{2,1,0:T(8,128)S(1)} copy-done((f32[8,16,128]{2,1,0:T(8,128)S(1)}, f32[8,16,128]{2,1,0:T(8,128)}, u32[]{:S(2)}) %copy-start.1) | copy-done | bytes 65560
  2.4 36.1 %shard_map.41 = (f32[128,128]{1,0:T(8,128)S(1)}, f32[128,128]{1,0:T(8,128)S(1)}) custom-call(f32[128,128]{1,0:T(8,128)S(1)} %bitcast.7, f32[384,128]{1,0:T(8,128)S(1)} %bitcast.4), custom_call_target="tpu_custom_call" | custom-call | tf_op jit(solution)/shard_map/pallas_call | solution.py:560
  38.5 0.6 %copy.6 = f32[8,16,128]{2,1,0:T(8,128)} copy(f32[8,16,128]{2,1,0:T(8,128)S(1)} %bitcast.6) | data formatting | bytes 131072
  39.1 0.6 %copy.7 = f32[8,16,128]{2,1,0:T(8,128)} copy(f32[8,16,128]{2,1,0:T(8,128)S(1)} %bitcast.5) | data formatting | bytes 131072
Async XLA Ops:
  0.6 0.9 %copy-start = (f32[3,8,16,128]{3,2,1,0:T(8,128)S(1)}, f32[3,8,16,128]{3,2,1,0:T(8,128)}, u32[]{:S(2)}) copy-start(f32[3,8,16,128]{3,2,1,0:T(8,128)} %param.3) | copy-start | bytes 589828
  1.6 0.8 %copy-start.1 = (f32[8,16,128]{2,1,0:T(8,128)S(1)}, f32[8,16,128]{2,1,0:T(8,128)}, u32[]{:S(2)}) copy-start(f32[8,16,128]{2,1,0:T(8,128)} %param.2) | copy-start | bytes 196612

commit v5 on v4

--- a/solution.py
+++ b/solution.py
@@ -152,15 +152,15 @@
     sends = []
     east, west = beside(1, 0), beside(-1, 0)
     rest = pl.ds(1, 3)
-    sends.append(send(e0.at[0, pl.ds(16, 8), 0], e0.at[0, pl.ds(0, 8), 0], r1_sem.at[0], east, 0))
-    sends.append(send(e0.at[0, pl.ds(8, 8), 0], e0.at[0, pl.ds(24, 8), 0], r1_sem.at[1], west, 1))
-    sends.append(send(e0.at[rest, pl.ds(18, 6), 0], e0.at[rest, pl.ds(2, 6), 0], r1_sem.at[2], east, 2))
-    sends.append(send(e0.at[rest, pl.ds(8, 6), 0], e0.at[rest, pl.ds(24, 6), 0], r1_sem.at[3], west, 3))
     for side, (packed, into) in enumerate(((kr, rkl), (kl, rkr))):
         dy = 1 - 2 * side
         for n, (dx, a, b, c) in enumerate(((1, 2, 2, 0), (-1, 0, 2, 6), (0, 0, 4, 2))):
             at = 4 + 3 * side + n
             sends.append(send(packed.at[pl.ds(a, b)], into.at[pl.ds(c, b)], r1_sem.at[at], beside(dx, dy), at))
+    sends.append(send(e0.at[0, pl.ds(16, 8), 0], e0.at[0, pl.ds(0, 8), 0], r1_sem.at[0], east, 0))
+    sends.append(send(e0.at[0, pl.ds(8, 8), 0], e0.at[0, pl.ds(24, 8), 0], r1_sem.at[1], west, 1))
+    sends.append(send(e0.at[rest, pl.ds(18, 6), 0], e0.at[rest, pl.ds(2, 6), 0], r1_sem.at[2], east, 2))
+    sends.append(send(e0.at[rest, pl.ds(8, 6), 0], e0.at[rest, pl.ds(24, 6), 0], r1_sem.at[3], west, 3))
     for n in range(4):
         pairs[n] = matrix_of(jnp.logical_or(source == goal, source == (goal ^ (1 << n))), 0.25)
     for comp in range(3):

time: 39.9 us -> 39.8 us (level)
  no operation moved by 1% of the time
where the time goes in v5:
time: 39.8 us; the launch traced here: 39.7 us
  Pallas kernels  36 us (90%)
  local copies, waits for them, and re-layouts  3.02 us (8%)
  between operations  0.65 us (2%)
    pallas_call x1, Pallas kernels, on_device(): pl.pallas_call(kernel, out_shape=(flat, flat), in_specs=[pl.BlockSpec(mem...  36 us
    unnamed x6, local copies, waits for them, and re-layouts  3.02 us

profile of v5, /device:TPU:1, one launch (start us, length us, event | category | flops | bytes accessed | tf_op | source)
XLA Modules:
  0.0 39.7 jit_solution(1330695452890887415)
XLA Ops:
  0.6 0.0 copy-start
  0.6 0.9 %copy-done = f32[3,8,16,128]{3,2,1,0:T(8,128)S(1)} copy-done((f32[3,8,16,128]{3,2,1,0:T(8,128)S(1)}, f32[3,8,16,128]{3,2,1,0:T(8,128)}, u32[]{:S(2)}) %copy-start) | copy-done | bytes 196632
  1.6 0.0 copy-start.1
  1.6 0.8 %copy-done.1 = f32[8,16,128]{2,1,0:T(8,128)S(1)} copy-done((f32[8,16,128]{2,1,0:T(8,128)S(1)}, f32[8,16,128]{2,1,0:T(8,128)}, u32[]{:S(2)}) %copy-start.1) | copy-done | bytes 65560
  2.4 36.0 %shard_map.41 = (f32[128,128]{1,0:T(8,128)S(1)}, f32[128,128]{1,0:T(8,128)S(1)}) custom-call(f32[128,128]{1,0:T(8,128)S(1)} %bitcast.7, f32[384,128]{1,0:T(8,128)S(1)} %bitcast.4), custom_call_target="tpu_custom_call" | custom-call | tf_op jit(solution)/shard_map/pallas_call | solution.py:560
  38.4 0.6 %copy.6 = f32[8,16,128]{2,1,0:T(8,128)} copy(f32[8,16,128]{2,1,0:T(8,128)S(1)} %bitcast.6) | data formatting | bytes 131072
  39.0 0.6 %copy.7 = f32[8,16,128]{2,1,0:T(8,128)} copy(f32[8,16,128]{2,1,0:T(8,128)S(1)} %bitcast.5) | data formatting | bytes 131072
Async XLA Ops:
  0.6 0.9 %copy-start = (f32[3,8,16,128]{3,2,1,0:T(8,128)S(1)}, f32[3,8,16,128]{3,2,1,0:T(8,128)}, u32[]{:S(2)}) copy-start(f32[3,8,16,128]{3,2,1,0:T(8,128)} %param.3) | copy-start | bytes 589828
  1.6 0.8 %copy-start.1 = (f32[8,16,128]{2,1,0:T(8,128)S(1)}, f32[8,16,128]{2,1,0:T(8,128)}, u32[]{:S(2)}) copy-start(f32[8,16,128]{2,1,0:T(8,128)} %param.2) | copy-start | bytes 196612
